TPU v7x, 128 devices: a whole 4x4x4 slice. The times are simulated.
128 devices in a mesh: tm: 16 (over x_lo, y, core), chan: 8 (over z, x_hi).
Axes of the slice: x: 4 (x_hi: 2, x_lo: 2; x = x_hi * 2 + x_lo), y: 4, z: 4, core: 2. Of those that a mesh axis runs over, the one named last changes fastest.
Arguments:
- frames: bfloat16 [32768, 1280], P('tm', 'chan'), may hold values from -64 to 64
- up_weight: bfloat16 [1280, 5120], P('tm', 'chan'), may hold values from -0.15625 to 0.15625
- down_weight: bfloat16 [5120, 1280], P('chan', 'tm'), may hold values from -0.078125 to 0.078125
- ffn_gain: float32 [1280], replicated, may hold values from 0.1 to 1.9
- final_gain: float32 [1280], replicated, may hold values from 0.5 to 1.5
- ctc_weight: bfloat16 [1280, 256], replicated, may hold values from -12 to 12
- labels: int32 [8192], replicated, may hold values from 0 to 255, as said below
- starts: int32 [128], replicated, may hold values from 0 to 7936, as said below
- widths: int32 [128], replicated, may hold values from 64 to 128
Outputs:
- emissions: float32 [32768, 256], P(('tm', 'chan'))
- band_scores: float32 [128, 128], P(('tm', 'chan'))
Inputs may be any that keep to these rules, and one draw needn't show every extreme that they name: `labels`: every even state has id 0. Never falling; starts[0] and each rise from one entry to the next are at most 128; the last entry is the largest.
All inputs are finite; a program needn't handle non-finite values.
Results may differ from a plain program's by a relative error of at most 0.0023.
Values may be sent and summed in bfloat16 or wider, within the bound.
A program may use at most 64 MiB of HBM per device.

v0:
```python
import jax
import jax.numpy as jnp
from jax import lax
from jax.sharding import PartitionSpec as P

D = 1280
BAND = 128


LN_EPSILON = 1e-05
NEG_SCORE = -1000000000.0


def carried_in(x, axis, combine, identity):
    size, mine = (lax.axis_size(axis), lax.axis_index(axis))
    everything = lax.all_gather(x, axis)
    start = jnp.broadcast_to(jnp.asarray(identity, x.dtype), x.shape)

    def lap(k, before):
        reached = k < mine
        new = combine(before, everything[k])
        return jnp.where(reached, new, before)

    return lax.fori_loop(0, size, lap, start)


def norm_rows(values, gain_row):
    row_mean = jnp.mean(values, axis=-1, keepdims=True)
    row_var = jnp.mean(jnp.square(values - row_mean), axis=-1, keepdims=True)
    return (values - row_mean) * lax.rsqrt(row_var + LN_EPSILON) * gain_row


def max_plus(earlier, later):
    return jnp.max(earlier[:, :, None] + later[None, :, :], axis=1)


def block_hidden(frames, up_weight, ffn_gain):
    gathered = lax.all_gather(frames, "chan", axis=1, tiled=True)
    normed_in = norm_rows(gathered.astype(jnp.float32), ffn_gain).astype(jnp.bfloat16)
    pre_act = jnp.dot(
        normed_in,
        lax.all_gather(up_weight, "tm", axis=0, tiled=True),
        preferred_element_type=jnp.float32,
    )
    return (gathered, jax.nn.silu(pre_act).astype(jnp.bfloat16))


def local(frames, up_weight, down_weight, ffn_gain, final_gain, ctc_weight, labels, starts, widths):
    chan_count = lax.axis_size("chan")
    chan_pos = lax.axis_index("chan")
    frames_dev = frames.shape[0] // chan_count
    gathered, hidden = block_hidden(frames, up_weight, ffn_gain)
    partial_terms = jnp.dot(
        hidden,
        lax.all_gather(down_weight, "tm", axis=1, tiled=True),
        preferred_element_type=jnp.float32,
    )
    summed = lax.psum_scatter(partial_terms, "chan", scatter_dimension=1, tiled=True)
    residual = frames.astype(jnp.float32) + 0.5 * summed
    width_dev = frames.shape[1]
    totals, squares = lax.psum(
        (jnp.sum(residual, axis=1), jnp.sum(residual * residual, axis=1)), "chan"
    )
    row_mean = totals / D
    row_var = squares / D - row_mean * row_mean
    gain_dev = lax.dynamic_slice_in_dim(final_gain, chan_pos * width_dev, width_dev)
    normed = (
        (residual - row_mean[:, None]) * lax.rsqrt(row_var + LN_EPSILON)[:, None] * gain_dev
    ).astype(jnp.bfloat16)
    weight_dev = lax.dynamic_slice_in_dim(ctc_weight, chan_pos * width_dev, width_dev, 0)
    partial_value = jnp.dot(normed, weight_dev, preferred_element_type=jnp.float32)
    logits = lax.psum_scatter(partial_value, "chan", scatter_dimension=0, tiled=True)
    emissions = jax.nn.log_softmax(logits, axis=-1)
    shard_index = lax.axis_index("tm") * chan_count + chan_pos
    scale_out = 1.0 / (frames_dev * chan_count * lax.axis_size("tm"))
    band_index = jnp.arange(BAND, dtype=jnp.int32)
    window = jnp.arange(2 * BAND, dtype=jnp.int32)
    prior_shard = jnp.maximum(shard_index - 1, 0)
    start_in = jnp.where(shard_index > 0, starts[prior_shard], 0)
    width_in = jnp.where(shard_index > 0, widths[prior_shard], 2)
    window_ids = lax.dynamic_slice_in_dim(labels, start_in, 2 * BAND)
    before = jnp.concatenate([jnp.full((2,), -1, jnp.int32), window_ids[:-2]])
    skip_ok = (window >= 2) & (window_ids != before)
    choose = (
        window_ids[None, :] == jnp.arange(emissions.shape[1], dtype=jnp.int32)[:, None]
    ).astype(jnp.float32)
    scores = jnp.dot(
        emissions, choose, precision=lax.Precision.HIGHEST, preferred_element_type=jnp.float32
    )
    path_state = jnp.where(
        (window[None, :] == band_index[:, None]) & (band_index[:, None] < width_in), 0.0, NEG_SCORE
    ).astype(jnp.float32)
    frame_groups = scores.reshape(frames_dev // 32, 32, 2 * BAND)

    def frame_step(path_state, frame_emit):
        from_one = jnp.concatenate(
            [jnp.full((BAND, 1), NEG_SCORE, jnp.float32), path_state[:, :-1]], axis=1
        )
        from_two = jnp.concatenate(
            [jnp.full((BAND, 2), NEG_SCORE, jnp.float32), path_state[:, :-2]], axis=1
        )
        from_two = jnp.where(skip_ok[None, :], from_two, NEG_SCORE)
        return jnp.maximum(jnp.maximum(path_state, from_one), from_two) + frame_emit[None, :]

    def advance(path_state, group_emit):
        for frame_pos in range(32):
            path_state = frame_step(path_state, group_emit[frame_pos])
        return (path_state, None)

    path_state, _ = lax.scan(advance, path_state, frame_groups)
    offset = starts[shard_index] - start_in
    transfer = lax.dynamic_slice_in_dim(path_state, offset, BAND, 1)
    live_cols = band_index < widths[shard_index]
    transfer = jnp.where(live_cols[None, :], transfer, NEG_SCORE)
    identity = jnp.where(band_index[:, None] == band_index[None, :], 0.0, NEG_SCORE).astype(
        jnp.float32
    )
    prefix = carried_in(transfer, ("tm", "chan"), max_plus, identity)
    entry_scores = jnp.max(prefix, axis=0)
    exit_scores = jnp.max(entry_scores[:, None] + transfer, axis=0)
    band_row = jnp.where(live_cols, exit_scores * scale_out, 0.0)
    return (emissions, band_row[None, :])


def solution(mesh):
    in_specs = (P("tm", "chan"), P("tm", "chan"), P("chan", "tm"), P(), P(), P(), P(), P(), P())
    out_specs = (P(("tm", "chan"), None), P(("tm", "chan"), None))
    return jax.shard_map(local, mesh=mesh, in_specs=in_specs, out_specs=out_specs, check_vma=False)
```

profile of v0, /device:TPU:27, one launch (start us, length us, event | category | flops | bytes accessed | tf_op | source)
XLA Modules:
  0.0 1429.3 jit_solution(11404498909085422775)
XLA Ops:
  9.5 82.0 %all-gather.6.cloned.1.call-done = bf16[2048,1280]{0,1:T(8,128)(2,1)} async-done(((bf16[2048,160]{0,1:T(8,128)(2,1)}), bf16[2048,1280]{0,1:T(8,128)(2,1)}) %all-gather.6.cloned.1.call-update) | async-done | bytes 5242896 | tf_op jit(solution)/shard_map/all_gather | solution.py:38
  96.9 27.3 %all-gather.10.cloned.1.call-done = bf16[640,1280]{0,1:T(8,128)(2,1)} async-done(((bf16[640,80]{0,1:T(8,128)(2,1)}), bf16[640,1280]{0,1:T(8,128)(2,1)}) %all-gather.10.cloned.1.call-update) | async-done | bytes 1638416 | tf_op jit(solution)/shard_map/all_gather | solution.py:55
  124.3 35.1 %all-gather.8.cloned.1.call-done = bf16[1280,640]{1,0:T(8,128)(2,1)} async-done(((bf16[80,640]{1,0:T(8,128)(2,1)}), bf16[1280,640]{1,0:T(8,128)(2,1)}) %all-gather.8.cloned.1.call-update) | async-done | bytes 1638416 | tf_op jit(solution)/shard_map/all_gather | solution.py:42
  159.4 15.8 %fusion.10 = f32[2048,1280]{0,1:T(8,128)} fusion(bf16[640,1280]{0,1:T(8,128)(2,1)} %all-gather.10.cloned.1.call-done, bf16[1280,640]{1,0:T(8,128)(2,1)} %all-gather.8.cloned.1.call-done, bf16[2048,1280]{0,1:T(8,128)(2,1)} %all-gather.6.cloned.1.call-done, f32[1280]{0:T(1024)S(1)} %copy-done.6, f32[2048]{0:T(1024)S(1)} %add_rsqrt_fusion.1, ...), kind=kOutput, calls=%fused_computation.79 | convolution fusion | flops 6730547200 | bytes 19026944 | tf_op jit(solution)/shard_map/dot_general | solution.py:53
  176.1 132.0 %reduce-scatter.3.cloned.1.call-done = f32[2048,160]{0,1:T(8,128)} async-done(((f32[2048,1280]{0,1:T(8,128)}), f32[2048,160]{0,1:T(8,128)}) %reduce-scatter.3.cloned.1.call-update) | async-done | bytes 1310736 | tf_op jit(solution)/shard_map/reduce_scatter | solution.py:58
  309.7 31.2 %all-reduce.65 = (f32[2048]{0:T(1024)S(1)}, f32[2048]{0:T(1024)S(1)}) all-reduce(f32[2048]{0:T(1024)S(1)} %get-tuple-element.106, f32[2048]{0:T(1024)S(1)} %get-tuple-element.105), channel_id=1, replica_groups=mesh['tm'=16,'chan'=8] {'chan'}, use_global_device_ids=true, to_apply=%region_6.7 | all-reduce | flops 4096 | bytes 32768 | tf_op jit(solution)/shard_map/psum | solution.py:61
  349.4 72.7 %reduce-scatter.5.cloned.1.call-done = f32[256,256]{1,0:T(8,128)} async-done(((f32[2048,256]{1,0:T(8,128)}), f32[256,256]{1,0:T(8,128)}) %reduce-scatter.5.cloned.1.call-update) | async-done | bytes 262160 | tf_op jit(solution)/shard_map/reduce_scatter | solution.py:72
  426.2 38.0 %while.23 = (s32[]{:T(128)}, f32[128,256]{1,0:T(8,128)S(1)}, pred[256]{0:T(512)(128)(4,1)S(1)}, f32[8,32,256]{2,1,0:T(8,128)S(1)}, s32[]{:T(128)}, /*index=5*/s3...) while((s32[]{:T(128)}, f32[128,256]{1,0:T(8,128)S(1)}, ...), condition=%wide.region_11.12_spmd, body=%wide.region_10.11_spmd.sunk | while | flops 4194337 | bytes 16835380 | solution.py:110
  465.0 312.0 %all-gather.12.cloned.1.call-done = f32[16384,128]{1,0:T(8,128)} async-done(((f32[128,128]{1,0:T(8,128)}), f32[16384,128]{1,0:T(8,128)}) %all-gather.12.cloned.1.call-update) | async-done | bytes 8388624 | tf_op jit(solution)/shard_map/all_gather | solution.py:16
  777.0 644.0 %while.24 = (s32[]{:T(128)}, f32[128,128]{1,0:T(8,128)S(1)}, s32[]{:T(128)}, f32[128,128,128]{2,1,0:T(8,128)}, s32[]{:T(128)}) while((s32[]{:T(128)}, f32[128,128]{1,0:T(8,128)S(1)}, s32[]{:T(128)}, f32[128,128,128]{2,1,0:T(8,128)}, s32[]{:T(128)}) %tuple.104), condition=%wide.region_14.15_spmd, body=%wide.region_12.14_spmd.sunk | while | flops 4194307 | bytes 524363 | solution.py:24
  777.9 4.1 add_reduce_fusion.3
  782.9 4.1 add_reduce_fusion.3
  787.9 4.1 add_reduce_fusion.3
  793.0 4.1 add_reduce_fusion.3
  798.0 4.1 add_reduce_fusion.3
  803.0 4.1 add_reduce_fusion.3
  848.3 4.1 add_reduce_fusion.3
  853.4 4.1 add_reduce_fusion.3
  858.4 4.1 add_reduce_fusion.3
  863.4 4.1 add_reduce_fusion.3
  868.4 4.1 add_reduce_fusion.3
  873.5 4.1 add_reduce_fusion.3
  878.5 4.1 add_reduce_fusion.3
  883.5 4.1 add_reduce_fusion.3
  (692 shorter events, 640.4 us)
Async XLA Ops:
  7.2 333.8 %copy-start = (bf16[1280,256]{1,0:T(8,128)(2,1)S(1)}, bf16[1280,256]{1,0:T(8,128)(2,1)}, u32[]{:S(2)}) copy-start(bf16[1280,256]{1,0:T(8,128)(2,1)} %param.18) | copy-start | bytes 1966084
  7.2 84.3 %all-gather.6.cloned.1.call-start = ((), (), s32[]{:S(2)}) async-start(), calls=%async_computation.2 | async-start | bytes 5898240 | tf_op jit(solution)/shard_map/all_gather | solution.py:38
  7.9 116.3 %all-gather.10.cloned.1.call-start = ((), (), s32[]{:S(2)}) async-start(), calls=%async_computation.4 | async-start | bytes 1740800 | tf_op jit(solution)/shard_map/all_gather | solution.py:55
  8.7 150.7 %all-gather.8.cloned.1.call-start = ((), (), s32[]{:S(2)}) async-start(), calls=%async_computation.3 | async-start | bytes 1740800 | tf_op jit(solution)/shard_map/all_gather | solution.py:42
  9.4 150.0 %copy-start.6 = (f32[1280]{0:T(1024)S(1)}, f32[1280]{0:T(1024)}, u32[]{:S(2)}) copy-start(f32[1280]{0:T(1024)} %param.16) | copy-start | bytes 15364
  9.4 298.7 %reduce-scatter.3.cloned.1.call-start = ((), (), s32[]{:S(2)}) async-start(), calls=%async_computation.5 | async-start | bytes 11796480 | tf_op jit(solution)/shard_map/reduce_scatter | solution.py:58
  91.4 4.0 copy-start.1
  175.2 132.9 %copy-start.2 = (bf16[2048,160]{0,1:T(8,128)(2,1)S(1)}, bf16[2048,160]{0,1:T(8,128)(2,1)}, u32[]{:S(2)}) copy-start(bf16[2048,160]{0,1:T(8,128)(2,1)} %param.13) | copy-start | bytes 1966084
  175.2 169.2 %copy-start.4 = (s32[128]{0:T(128)S(1)}, s32[128]{0:T(128)}, u32[]{:S(2)}) copy-start(s32[128]{0:T(128)} %param.21) | copy-start | bytes 1540
  175.2 169.2 %copy-start.5 = (s32[128]{0:T(128)S(1)}, s32[128]{0:T(128)}, u32[]{:S(2)}) copy-start(s32[128]{0:T(128)} %param.20) | copy-start | bytes 1540
  175.2 246.9 %reduce-scatter.5.cloned.1.call-start = ((), (), s32[]{:S(2)}) async-start(), calls=%async_computation.6 | async-start | bytes 2359296 | tf_op jit(solution)/shard_map/reduce_scatter | solution.py:72
  344.2 432.8 %all-gather.12.cloned.1.call-start = ((), (), s32[]{:S(2)}) async-start(), calls=%async_computation.7 | async-start | bytes 8454144 | tf_op jit(solution)/shard_map/all_gather | solution.py:16
  425.5 0.7 copy-start.3
Sparse Core Ops, SparseCore 0:
  10.3 81.0 all-gather.5
  93.1 31.0 all-gather.9
  126.0 33.3 all-gather.7
  175.3 132.7 reduce-scatter.2
  344.3 77.8 reduce-scatter.4
  465.1 311.8 all-gather.11
where the time goes:
time: 1440 us; the launch traced here: 1430 us
  waiting for transfers between devices  663 us (46%)
  other arithmetic  579 us (40%)
  local copies, waits for them, and re-layouts  113 us (8%)
  blocking collectives  31.2 us (2%)
  matrix products  19.4 us (1%)
  between operations  16.2 us (1%)
    reduce_max x128, other arithmetic, max_plus(): return jnp.max(earlier[:, :, None] + later[None, :, :], axis=1)  529 us
    all_gather x1, waiting for transfers between devices, carried_in(): everything = lax.all_gather(x, axis)  312 us
    reduce_scatter x1, waiting for transfers between devices, local(): lax.psum_scatter(partial_terms, 'chan', scatter_dimension=1, tiled=True)  132 us
    add x128, local copies, waits for them, and re-layouts, max_plus(): return jnp.max(earlier[:, :, None] + later[None, :, :], axis=1)  109 us
    all_gather x1, waiting for transfers between devices, block_hidden(): gathered = lax.all_gather(frames, 'chan', axis=1, tiled=True)  82 us
    reduce_scatter x1, waiting for transfers between devices, local(): lax.psum_scatter(partial_value, 'chan', scatter_dimension=0, tiled=True)  72.7 us
    all_gather x1, waiting for transfers between devices, block_hidden(): lax.all_gather(up_weight, 'tm', axis=0, tiled=True)  35.1 us
    add x256, other arithmetic, frame_step(): jnp.maximum(jnp.maximum(path_state, from_one), from_two)  34.5 us
  transfers between devices with their start and end apart: 6, of which 6 were waited for; matrix products, arithmetic and copies ran while one was open for 1% of the time, Pallas kernels for 0%

commit v1 on v0

v1 whole, which is shorter than its diff:
```python
import functools

import jax
import jax.numpy as jnp
from jax import lax
from jax.experimental import pallas as pl
from jax.experimental.pallas import tpu as pltpu
from jax.sharding import PartitionSpec as P

BAND = 128
LN_EPSILON = 1e-05
NEG = -1e30
MESH = pl.DeviceIdType.MESH
ANY = pl.BlockSpec(memory_space=pl.ANY)
VM = pl.BlockSpec(memory_space=pltpu.VMEM)
MIB = 2**20


def position():
    tm, chan = lax.axis_index("tm"), lax.axis_index("chan")
    x = lax.rem(chan, 2) * 2 + tm // 8
    return x, lax.rem(tm // 2, 4), chan // 2, lax.rem(tm, 2)


def device(x, y, z, core):
    return (lax.rem(x, 2) * 8 + y * 2 + core, z * 2 + x // 2)


def moved(pos, axis, by):
    out = list(pos)
    out[axis] = lax.rem(pos[axis] + by + 4, 4)
    return tuple(out)


PARTS = ((0, 64, (2, 0, 1)), (64, 48, (1, 2, 0)), (112, 48, (0, 1, 2)))
STEPS = (0, -1, 1, 2)


def block_at(w, pos, part):
    x, y, z, core = pos
    row, rows, _ = part
    return w.at[z, x // 2, lax.rem(x, 2), y, core, pl.ds(row, rows)]


def column_at(w, pos, part):
    x, y, z, core = pos
    row, rows, (axis, _, _) = part
    if axis == 0:
        return w.at[z, :, :, y, core, pl.ds(row, rows)]
    if axis == 1:
        return w.at[z, x // 2, lax.rem(x, 2), :, core, pl.ds(row, rows)]
    return w.at[:, x // 2, lax.rem(x, 2), y, core, pl.ds(row, rows)]


def gather_kernel(frames, chunk, w, mine, local_sem, fr_send, fr_recv, s1, r1, s2, r2, s3, r3, sc, rc):
    me = position()
    x, y, z, core = me
    tm, chan = lax.axis_index("tm"), lax.axis_index("chan")
    sibling = (tm + 1 - 2 * core, chan)

    barrier = pltpu.get_barrier_semaphore()
    for axis in range(3):
        for by in (1, -1):
            pl.semaphore_signal(barrier, inc=1, device_id=device(*moved(me, axis, by)), device_id_type=MESH)
    pl.semaphore_signal(barrier, inc=1, device_id=sibling, device_id_type=MESH)
    for d in range(1, 8):
        pl.semaphore_signal(barrier, inc=1, device_id=(tm, lax.rem(chan + d, 8)), device_id_type=MESH)
    pl.semaphore_wait(barrier, 14)

    pending = []

    def send(src, dst, send_sem, recv_sem, to):
        copy = pltpu.make_async_remote_copy(
            src_ref=src, dst_ref=dst, send_sem=send_sem, recv_sem=recv_sem, device_id=to, device_id_type=MESH
        )
        copy.start()
        pending.append(copy)

    def arrived(ref, sem):
        pltpu.make_async_copy(ref, ref, sem).wait()

    own = pltpu.make_async_copy(chunk, w.at[z, x // 2, lax.rem(x, 2), y, core], local_sem.at[0])
    own.start()
    for d in range(1, 8):
        peer = lax.rem(chan + d, 8)
        send(
            frames.at[pl.ds(peer * 256, 256)], mine.at[chan], fr_send.at[d - 1], fr_recv.at[d - 1], (tm, peer)
        )
    own_frames = pltpu.make_async_copy(frames.at[pl.ds(chan * 256, 256)], mine.at[chan], local_sem.at[1])
    own_frames.start()
    own.wait()

    def to_sibling(p, k, ref):
        send(ref, ref, sc.at[p, k], rc.at[p, k], sibling)

    def phase_sends(ref, axis, send_sems, recv_sems):
        send(ref, ref, send_sems(0), recv_sems(1), device(*moved(me, axis, 1)))
        send(ref, ref, send_sems(1), recv_sems(2), device(*moved(me, axis, -1)))

    for p, part in enumerate(PARTS):
        block = block_at(w, me, part)
        phase_sends(block, part[2][0], lambda k: s1.at[p, k], lambda k: r1.at[p, k])
        phase_sends(block, part[2][1], lambda k: s2.at[p, 0, k], lambda k: r2.at[p, 0, k])
    for k in (1, 2, 3):
        for p, part in enumerate(PARTS):
            a, b, _ = part[2]
            at = moved(me, a, STEPS[k])
            block = block_at(w, at, part)
            arrived(block, r1.at[p, k])
            if k == 1 + p % 2:
                send(block, block, s1.at[p, 2], r1.at[p, 3], device(*moved(me, a, -STEPS[k])))
            phase_sends(block, b, lambda q: s2.at[p, k, q], lambda q: r2.at[p, k, q])
    for p, part in enumerate(PARTS):
        column = column_at(w, me, part)
        phase_sends(column, part[2][2], lambda q: s3.at[p, 0, q], lambda q: r3.at[p, 0, q])
        to_sibling(p, 0, column)
    for j in (1, 2, 3):
        for p, part in enumerate(PARTS):
            a, b, c = part[2]
            for k in range(4):
                at = moved(moved(me, b, STEPS[j]), a, STEPS[k])
                block = block_at(w, at, part)
                arrived(block, r2.at[p, k, j])
                if j == 1 + k % 2:
                    send(block, block, s2.at[p, k, 2], r2.at[p, k, 3], device(*moved(me, b, -STEPS[j])))
            column = column_at(w, moved(me, b, STEPS[j]), part)
            phase_sends(column, c, lambda q: s3.at[p, j, q], lambda q: r3.at[p, j, q])
            to_sibling(p, j, column)
    for i in (1, 2, 3):
        for j in range(4):
            for p, part in enumerate(PARTS):
                _, b, c = part[2]
                column = column_at(w, moved(moved(me, c, STEPS[i]), b, STEPS[j]), part)
                arrived(column, r3.at[p, j, i])
                if i == 1 + j % 2:
                    send(column, column, s3.at[p, j, 2], r3.at[p, j, 3], device(*moved(me, c, -STEPS[i])))
                to_sibling(p, 4 * i + j, column)
    other = (x, y, z, 1 - core)
    for i in range(4):
        for j in range(4):
            for p, part in enumerate(PARTS):
                _, b, c = part[2]
                column = column_at(w, moved(moved(other, c, STEPS[i]), b, STEPS[j]), part)
                arrived(column, rc.at[p, 4 * i + j])
    own_frames.wait()
    for d in range(1, 8):
        src = lax.rem(chan + 8 - d, 8)
        arrived(mine.at[src], fr_recv.at[d - 1])
    for copy in pending:
        copy.wait_send()


def gather(frames, chunk):
    dma = pltpu.SemaphoreType.DMA
    return pl.pallas_call(
        gather_kernel,
        out_shape=(
            jax.ShapeDtypeStruct((4, 2, 2, 4, 2, 160, 640), jnp.bfloat16),
            jax.ShapeDtypeStruct((8, 256, 160), jnp.bfloat16),
        ),
        in_specs=[ANY, ANY],
        out_specs=(ANY, ANY),
        scratch_shapes=[
            dma((2,)), dma((7,)), dma((7,)),
            dma((3, 3)), dma((3, 4)),
            dma((3, 4, 3)), dma((3, 4, 4)),
            dma((3, 4, 3)), dma((3, 4, 4)),
            dma((3, 16)), dma((3, 16)),
        ],
        compiler_params=pltpu.CompilerParams(collective_id=1, has_side_effects=True),
        name="gather",
    )(frames, chunk)


def norm_rows(values, gain_row):
    row_mean = jnp.mean(values, axis=-1, keepdims=True)
    centred = values - row_mean
    row_var = jnp.mean(jnp.square(centred), axis=-1, keepdims=True)
    return centred * lax.rsqrt(row_var + LN_EPSILON) * gain_row


def split(values):
    high = values.astype(jnp.bfloat16)
    return high, (values - high.astype(jnp.float32)).astype(jnp.bfloat16)


NT = (((1,), (1,)), ((), ()))


def viterbi(scal, emissions, ids, states):
    par, width_in, offset, width_out = scal[0], scal[1], scal[2], scal[3]
    char = lax.broadcasted_iota(jnp.int32, (128, 256), 1)
    choose = (ids[:, 0:1] == char).astype(jnp.float32) - (char == 0).astype(jnp.float32)
    choose = choose.astype(jnp.bfloat16)
    parts = list(split(emissions))
    parts.append((emissions - parts[0].astype(jnp.float32) - parts[1].astype(jnp.float32)).astype(jnp.bfloat16))
    gain = sum(lax.dot_general(choose, part, NT, preferred_element_type=jnp.float32) for part in parts)
    blank = jnp.sum(emissions[:, 0:1])
    skip = jnp.broadcast_to(jnp.where(ids[:, 0:1] == ids[:, 1:2], NEG, 0.0), (128, 128)).reshape(16, 8, 128)
    v = lax.broadcasted_iota(jnp.int32, (16, 8, 128), 0)
    sub = lax.broadcasted_iota(jnp.int32, (16, 8, 128), 1)
    start = lax.broadcasted_iota(jnp.int32, (16, 8, 128), 2)
    at = 2 * (sub * 16 + v) - par
    live = start < width_in
    even = jnp.where((at == start) & live, 0.0, NEG)
    odd = jnp.where((at + 1 == start) & live, 0.0, NEG)
    top = jnp.full((8, 128), NEG, jnp.float32)
    first = lax.broadcasted_iota(jnp.int32, (8, 128), 0) == 0
    for half in range(2):
        block = gain[:, half * 128 : half * 128 + 128].reshape(16, 8, 128)
        for t in range(128):
            step = jnp.broadcast_to(block[:, :, t : t + 1], (16, 8, 128))
            turned = pltpu.roll(odd[15], 1, 0)
            below = jnp.concatenate([jnp.where(first, NEG, turned)[None], odd[:15]], axis=0)
            top = jnp.maximum(top, turned)
            odd = jnp.maximum(jnp.maximum(odd, even), below + skip) + step
            even = jnp.maximum(even, below)
    for k in range(16):
        states[pl.ds(2 * k, 8, stride=32), :] = even[k]
        states[pl.ds(2 * k + 1, 8, stride=32), :] = odd[k]
    states[256:264, :] = top
    reached = states[pl.ds(par + offset, 128), :]
    row = lax.broadcasted_iota(jnp.int32, (128, 128), 0)
    reached = jnp.where(row < width_out, reached + blank, NEG)
    return jnp.transpose(reached)


def local_kernel(scal, w, mine, ffn_gain, final_gain, ctc, ids, emis, transfer, x_in, normed_in, total, states):
    step = pl.program_id(0)

    @pl.when(step == 0)
    def _():
        x_in[...] = jnp.concatenate([mine[k].astype(jnp.float32) for k in range(8)], axis=1)
        normed_in[...] = norm_rows(x_in[...], ffn_gain[...]).astype(jnp.bfloat16)
        total[...] = jnp.zeros_like(total)

    up = w[0, 0, :, :, :, 0:80, :].reshape(1280, 640)
    down = w[0, 0, :, :, :, 80:160, :].reshape(1280, 640)
    pre = jnp.dot(normed_in[...], up, preferred_element_type=jnp.float32)
    hidden = (pre / (1.0 + jnp.exp(-pre))).astype(jnp.bfloat16)
    total[...] += lax.dot_general(hidden, down, NT, preferred_element_type=jnp.float32)

    @pl.when(step == 7)
    def _():
        residual = x_in[...] + 0.5 * total[...]
        normed = norm_rows(residual, final_gain[...]).astype(jnp.bfloat16)
        logits = jnp.dot(normed, ctc[...], preferred_element_type=jnp.float32)
        shifted = logits - jnp.max(logits, axis=-1, keepdims=True)
        out = shifted - jnp.log(jnp.sum(jnp.exp(shifted), axis=-1, keepdims=True))
        emis[...] = out
        transfer[...] = viterbi(scal, out, ids[...], states)


def local_part(scal, w, mine, ffn_gain, final_gain, ctc, ids):
    whole = lambda *dims: pl.BlockSpec(dims, lambda i, s: (0,) * len(dims))
    return pl.pallas_call(
        local_kernel,
        out_shape=(jax.ShapeDtypeStruct((256, 256), jnp.float32), jax.ShapeDtypeStruct((128, 128), jnp.float32)),
        grid_spec=pltpu.PrefetchScalarGridSpec(
            num_scalar_prefetch=1,
            grid=(8,),
            in_specs=[
                pl.BlockSpec((1, 1, 2, 4, 2, 160, 640), lambda i, s: (i // 2, i % 2, 0, 0, 0, 0, 0)),
                whole(8, 256, 160), whole(1, 1280), whole(1, 1280), whole(1280, 256), whole(128, 2),
            ],
            out_specs=(whole(256, 256), whole(128, 128)),
            scratch_shapes=[
                pltpu.VMEM((256, 1280), jnp.float32),
                pltpu.VMEM((256, 1280), jnp.bfloat16),
                pltpu.VMEM((256, 1280), jnp.float32),
                pltpu.VMEM((400, 128), jnp.float32),
            ],
        ),
        compiler_params=pltpu.CompilerParams(vmem_limit_bytes=40 * MIB, dimension_semantics=("arbitrary",)),
        name="local_part",
    )(scal, w, mine, ffn_gain, final_gain, ctc, ids)


def row_to_column(row):
    i = lax.broadcasted_iota(jnp.int32, (128, 128), 0)
    j = lax.broadcasted_iota(jnp.int32, (128, 128), 1)
    return jnp.max(jnp.where(i == j, jnp.broadcast_to(row, (128, 128)), 4 * NEG), axis=1, keepdims=True)


def advance(column, matrix):
    return jnp.max(column + matrix, axis=0, keepdims=True)


def prefix_kernel(transfer, out, group, rows, spans, entry, entries, ts, tr, ps, pr, es, er, local_sem):
    tm, chan = lax.axis_index("tm"), lax.axis_index("chan")
    root = tm == 0
    barrier = pltpu.get_barrier_semaphore()
    for d in range(1, 8):
        pl.semaphore_signal(barrier, inc=1, device_id=(tm, lax.rem(chan + d, 8)), device_id_type=MESH)

    @pl.when(root)
    def _():
        def greet(k, carry):
            g, c = k // 8, lax.rem(k, 8)

            @pl.when(jnp.logical_or(g != tm, c != chan))
            def _():
                pl.semaphore_signal(barrier, inc=1, device_id=(g, c), device_id_type=MESH)

            return carry

        lax.fori_loop(0, 128, greet, 0)
        pl.semaphore_wait(barrier, 7 + 7 + 15)

    @pl.when(jnp.logical_not(root))
    def _():
        pl.semaphore_signal(barrier, inc=1, device_id=(0, chan), device_id_type=MESH)
        pl.semaphore_wait(barrier, 7 + 8)

    copies = []
    for d in range(1, 8):
        copy = pltpu.make_async_remote_copy(
            src_ref=transfer, dst_ref=group.at[chan], send_sem=ts.at[d - 1], recv_sem=tr.at[d - 1],
            device_id=(tm, lax.rem(chan + d, 8)), device_id_type=MESH,
        )
        copy.start()
        copies.append(copy)
    group[chan] = transfer[...]
    for copy in copies:
        copy.wait()

    span = group[0, pl.ds(pl.multiple_of(chan * 16, 16), 16), :]

    def grow(m, span):
        best = span[:, 0:1] + group[m, 0:1, :]
        for i in range(1, 128):
            best = jnp.maximum(best, span[:, i : i + 1] + group[m, i : i + 1, :])
        return best

    rows[...] = lax.fori_loop(1, 8, grow, span)

    mine = spans.at[tm, pl.ds(pl.multiple_of(chan * 16, 16), 16), :]
    for c in range(8):
        copy = pltpu.make_async_remote_copy(
            src_ref=rows, dst_ref=mine, send_sem=ps.at[c], recv_sem=pr.at[tm, chan],
            device_id=(0, c), device_id_type=MESH,
        )

        @pl.when(jnp.logical_not(jnp.logical_and(root, chan == c)))
        def _():
            copy.start()

        @pl.when(jnp.logical_and(root, chan == c))
        def _():
            same = pltpu.make_async_copy(rows, mine, local_sem)
            same.start()
            same.wait()

    @pl.when(root)
    def _():
        def await_rows(k, carry):
            g, c = k // 8, lax.rem(k, 8)
            here = spans.at[g, pl.ds(pl.multiple_of(c * 16, 16), 16), :]

            @pl.when(jnp.logical_or(g != tm, c != chan))
            def _():
                pltpu.make_async_copy(here, here, pr.at[g, c]).wait()

            return carry

        row = jnp.zeros((1, 128), jnp.float32)
        entry[...] = jnp.broadcast_to(row, (8, 128))
        lax.fori_loop(0, 128, await_rows, 0)

        def chain(g, row):
            row = advance(row_to_column(row), spans[g])
            entries[g] = jnp.broadcast_to(row, (8, 128))
            copy = pltpu.make_async_remote_copy(
                src_ref=entries.at[g], dst_ref=entry, send_sem=es.at[g], recv_sem=er,
                device_id=(g + 1, chan), device_id_type=MESH,
            )
            copy.start()
            return row

        lax.fori_loop(0, 15, chain, row)

        def sent(g, carry):
            pltpu.make_async_copy(entries.at[g], entries.at[g], es.at[g]).wait()
            return carry

        lax.fori_loop(0, 15, sent, 0)

    @pl.when(jnp.logical_not(root))
    def _():
        pltpu.make_async_copy(entry, entry, er).wait()

    row = lax.fori_loop(0, chan + 1, lambda m, row: advance(row_to_column(row), group[m]), entry[0:1, :])
    out[...] = jnp.where(row > 0.5 * NEG, row * (1.0 / 32768), 0.0)
    for c in range(8):

        @pl.when(jnp.logical_not(jnp.logical_and(root, chan == c)))
        def _():
            pltpu.make_async_copy(rows, rows, ps.at[c]).wait()


def prefix(transfer):
    dma = pltpu.SemaphoreType.DMA
    return pl.pallas_call(
        prefix_kernel,
        out_shape=jax.ShapeDtypeStruct((1, 128), jnp.float32),
        in_specs=[VM],
        out_specs=VM,
        scratch_shapes=[
            pltpu.VMEM((8, 128, 128), jnp.float32),
            pltpu.VMEM((16, 128), jnp.float32),
            pltpu.VMEM((16, 128, 128), jnp.float32),
            pltpu.VMEM((8, 128), jnp.float32),
            pltpu.VMEM((16, 8, 128), jnp.float32),
            dma((7,)), dma((7,)), dma((8,)), dma((16, 8)), dma((16,)), dma, dma,
        ],
        compiler_params=pltpu.CompilerParams(collective_id=2, has_side_effects=True),
        name="prefix",
    )(transfer)


def window_facts(labels, starts, widths):
    shard = lax.axis_index("tm") * 8 + lax.axis_index("chan")
    prior = jnp.maximum(shard - 1, 0)
    start_in = jnp.where(shard > 0, starts[prior], 0)
    width_in = jnp.where(shard > 0, widths[prior], 2)
    par = lax.rem(start_in, 2)
    base = start_in - par
    window = lax.dynamic_slice_in_dim(labels, base, 256)
    odd = window.reshape(128, 2)[:, 1]
    before = jnp.concatenate([jnp.full((1,), -1, jnp.int32), odd[:-1]])
    ids = jnp.stack([odd, before], axis=1).reshape(8, 16, 2).transpose(1, 0, 2).reshape(128, 2)
    scal = jnp.stack([par, width_in, starts[shard] - start_in, widths[shard]]).astype(jnp.int32)
    return scal, ids


def local(frames, up_weight, down_weight, ffn_gain, final_gain, ctc_weight, labels, starts, widths):
    scal, ids = window_facts(labels, starts, widths)
    chunk = jnp.concatenate([up_weight, down_weight.T], axis=0)
    w, mine = gather(frames, chunk)
    emissions, transfer = local_part(scal, w, mine, ffn_gain[None, :], final_gain[None, :], ctc_weight, ids)
    return emissions, prefix(transfer)


def solution(mesh):
    in_specs = (P("tm", "chan"), P("tm", "chan"), P("chan", "tm"), P(), P(), P(), P(), P(), P())
    out_specs = (P(("tm", "chan"), None), P(("tm", "chan"), None))
    return jax.shard_map(local, mesh=mesh, in_specs=in_specs, out_specs=out_specs, check_vma=False)
```

time: 1440 us -> 157 us (0.11)
  waiting for transfers between devices: 663 us -> 0 us
  other arithmetic: 579 us -> 2.45 us
  Pallas kernels: 0 us -> 140 us
  local copies, waits for them, and re-layouts: 113 us -> 10.6 us
  blocking collectives: 31.2 us -> 0 us
  matrix products: 19.4 us -> 0 us
    reduce_max x131 -> x0, other arithmetic: 530 us -> none  [the longest x128 529 us: max_plus(): return jnp.max(earlier[:, :, None] + later[None, :, :], axis=1)]
    all_gather x4 -> x0, waiting for transfers between devices: 456 us -> none  [the longest x1 312 us: carried_in(): everything = lax.all_gather(x, axis)]
    reduce_scatter x2 -> x0, waiting for transfers between devices: 205 us -> none  [the longest x1 132 us: local(): lax.psum_scatter(partial_terms, 'chan', scatter_dimension=1, tiled=True)]
    pallas_call x0 -> x3, Pallas kernels: none -> 140 us  [the longest x1 80.5 us: gather(): pl.pallas_call(gather_kernel, out_shape=(jax.ShapeDtypeStruct((4, 2, 2, 4...]
    add x128 -> x0, local copies, waits for them, and re-layouts: 109 us -> none  [max_plus(): return jnp.max(earlier[:, :, None] + later[None, :, :], axis=1)]
    add x256 -> x0, other arithmetic: 34.5 us -> none  [frame_step(): jnp.maximum(jnp.maximum(path_state, from_one), from_two)]
    psum x1 -> x0, blocking collectives: 31.2 us -> none  [local(): lax.psum((jnp.sum(residual, axis=1), jnp.sum(residual * residual, axis=1)...]
    dot_general x3 -> x0, matrix products: 19.4 us -> none  [the longest x1 15.8 us: local(): jnp.dot(hidden, lax.all_gather(down_weight, 'tm', axis=1, tiled=True), pr...]
  transfers between devices with their start and end apart: 6 -> 0, of which waited for: 6 -> 0; matrix products, arithmetic and copies ran while one was open for 1% -> 0% of each run, Pallas kernels for 0% -> 0%
where the time goes in v1:
time: 157 us; the launch traced here: 156 us
  Pallas kernels  140 us (89%)
  local copies, waits for them, and re-layouts  10.6 us (7%)
  between operations  2.55 us (2%)
  other arithmetic  2.45 us (2%)
    pallas_call x1, Pallas kernels, gather(): pl.pallas_call(gather_kernel, out_shape=(jax.ShapeDtypeStruct((4, 2, 2, 4...  80.5 us
    pallas_call x1, Pallas kernels, prefix(): pl.pallas_call(prefix_kernel, out_shape=jax.ShapeDtypeStruct((1, 128), jn...  35.8 us
    pallas_call x1, Pallas kernels, local_part(): pl.pallas_call(local_kernel, out_shape=(jax.ShapeDtypeStruct((256, 256),...  24 us
    unnamed x8, local copies, waits for them, and re-layouts  6.26 us

profile of v1, /device:TPU:27, one launch (start us, length us, event | category | flops | bytes accessed | tf_op | source)
XLA Modules:
  0.0 155.9 jit_solution(11116310003066073291)
XLA Ops:
  0.6 1.4 fusion
  3.9 0.7 pad_add_fusion.scal
  4.6 2.2 %copy.15.frames = bf16[2048,160]{1,0:T(8,128)(2,1)} copy(bf16[2048,160]{0,1:T(8,128)(2,1)} %param.9) | data formatting | bytes 1310720 | tf_op args[0]
  6.8 1.6 %pad_maximum_fusion.chunk = bf16[160,640]{1,0:T(8,128)(2,1)} fusion(bf16[80,640]{1,0:T(8,128)(2,1)} %bitcast.11, bf16[80,640]{1,0:T(8,128)(2,1)} %param.10), kind=kLoop, calls=%fused_computation | loop fusion | flops 409600 | bytes 409600 | tf_op jit(solution)/shard_map/concatenate | solution.py:438
  8.4 80.5 %gather.1 = (bf16[4,2,2,4,2,160,640]{6,5,4,3,2,1,0:T(8,128)(2,1)}, bf16[8,256,160]{2,1,0:T(8,128)(2,1)}) custom-call(bf16[2048,160]{1,0:T(8,128)(2,1)} %copy.15.frames, bf16[160,640]{1,0:T(8,128)(2,1)} %pad_maximum_fusion.chunk), custom_call_target="tpu_custom_call" | custom-call | tf_op jit(solution)/shard_map/gather/pallas_call | solution.py:155
  88.9 0.7 broadcast_in_dim.6.ffn_gain
  89.6 0.7 broadcast_in_dim.7.final_gain
  90.3 0.8 dynamic_slice.19
  91.1 0.1 reshape.15
  91.2 0.2 slice_reduce_fusion
  91.4 0.1 pad_add_fusion.1
  91.5 0.1 stack.25
  91.6 0.2 slice_reduce_fusion.1
  91.7 0.1 stack.24
  91.8 0.1 copy.16
  92.0 0.0 copy-start
  92.0 1.2 copy-done
  93.2 0.0 copy-start.1
  93.2 1.1 copy-done.1
  94.3 24.0 %local_part.1 = (f32[256,256]{1,0:T(8,128)}, f32[128,128]{1,0:T(8,128)S(1)}) custom-call(s32[4]{0:T(128)S(1)} %pad_add_fusion.scal, bf16[4,2,2,4,2,160,640]{6,5,4,3,2,1,0:T(8,128)(2,1)} %get-tuple-element.6.w, bf16[8,256,160]{2,1,0:T(8,128)(2,1)S(1)} %copy-done, f32[1,1280]{1,0:T(1,128)S(1)} %broadcast_in_dim.6.ffn_gain, ...), custom_call_target="tpu_custom_call" | custom-call | tf_op jit(solution)/shard_map/local_part/pallas_call | solution.py:256
  118.3 0.0 copy-start.2
  118.3 0.6 copy-done.2
  118.9 35.8 %prefix.1 = f32[1,128]{1,0:T(1,128)} custom-call(f32[128,128]{1,0:T(8,128)} %copy-done.2), custom_call_target="tpu_custom_call" | custom-call | tf_op jit(solution)/shard_map/prefix/pallas_call | solution.py:403
  154.8 1.1 copy.18
  (1 shorter events, 0.0 us)
Async XLA Ops:
  92.0 1.2 copy-start
  93.2 1.1 copy-start.1
  118.3 0.6 copy-start.2

commit v2 on v1

v2 whole, which is shorter than its diff:
```python
import functools

import jax
import jax.numpy as jnp
from jax import lax
from jax.experimental import pallas as pl
from jax.experimental.pallas import tpu as pltpu
from jax.sharding import PartitionSpec as P

BAND = 128
LN_EPSILON = 1e-05
NEG = -1e30
MESH = pl.DeviceIdType.MESH
ANY = pl.BlockSpec(memory_space=pl.ANY)
VM = pl.BlockSpec(memory_space=pltpu.VMEM)
MIB = 2**20


def position():
    tm, chan = lax.axis_index("tm"), lax.axis_index("chan")
    x = lax.rem(chan, 2) * 2 + tm // 8
    return x, lax.rem(tm // 2, 4), chan // 2, lax.rem(tm, 2)


def device(x, y, z, core):
    return (lax.rem(x, 2) * 8 + y * 2 + core, z * 2 + x // 2)


def moved(pos, axis, by):
    out = list(pos)
    out[axis] = lax.rem(pos[axis] + by + 4, 4)
    return tuple(out)


PARTS = ((0, 64, (2, 0, 1)), (64, 48, (1, 2, 0)), (112, 48, (0, 1, 2)))
STEPS = (0, -1, 1, 2)
NT = (((1,), (1,)), ((), ()))


def block_at(w, pos, part):
    x, y, z, core = pos
    row, rows, _ = part
    return w.at[z, x // 2, lax.rem(x, 2), y, core, pl.ds(row, rows)]


def column_at(w, pos, part):
    x, y, z, core = pos
    row, rows, (axis, _, _) = part
    if axis == 0:
        return w.at[z, :, :, y, core, pl.ds(row, rows)]
    if axis == 1:
        return w.at[z, x // 2, lax.rem(x, 2), :, core, pl.ds(row, rows)]
    return w.at[:, x // 2, lax.rem(x, 2), y, core, pl.ds(row, rows)]


def norm_rows(values, gain_row):
    row_mean = jnp.mean(values, axis=-1, keepdims=True)
    centred = values - row_mean
    row_var = jnp.mean(jnp.square(centred), axis=-1, keepdims=True)
    return centred * lax.rsqrt(row_var + LN_EPSILON) * gain_row


def gain_row(ref):
    return jnp.concatenate([ref[k : k + 1, :] for k in range(10)], axis=1)


def block_kernel(
    frames, up, down, ffn_gain, final_gain, ctc_hbm, emis,
    w, mine, ctc, x_in, normed_in, total,
    local_sem, fr_send, fr_recv, s1, r1, s2, r2, s0, r0, s3, r3, sc, rc,
):
    me = position()
    x, y, z, core = me
    tm, chan = lax.axis_index("tm"), lax.axis_index("chan")
    sibling = (tm + 1 - 2 * core, chan)

    barrier = pltpu.get_barrier_semaphore()
    for axis in range(3):
        for by in (1, -1):
            pl.semaphore_signal(barrier, inc=1, device_id=device(*moved(me, axis, by)), device_id_type=MESH)
    pl.semaphore_signal(barrier, inc=1, device_id=sibling, device_id_type=MESH)
    for d in range(1, 8):
        pl.semaphore_signal(barrier, inc=1, device_id=(tm, lax.rem(chan + d, 8)), device_id_type=MESH)
    here = w.at[z, x // 2, lax.rem(x, 2), y, core]
    locals_ = [
        pltpu.make_async_copy(up, here.at[pl.ds(0, 80)], local_sem.at[0]),
        pltpu.make_async_copy(down, here.at[pl.ds(80, 80)], local_sem.at[1]),
        pltpu.make_async_copy(frames.at[:, pl.ds(pl.multiple_of(chan * 256, 256), 256)], mine.at[chan], local_sem.at[2]),
        pltpu.make_async_copy(ctc_hbm, ctc, local_sem.at[3]),
    ]
    for copy in locals_:
        copy.start()
    locals_[0].wait()
    locals_[1].wait()
    pl.semaphore_wait(barrier, 14)

    pending = []

    def send(ref, send_sem, recv_sem, to, dst=None):
        copy = pltpu.make_async_remote_copy(
            src_ref=ref, dst_ref=ref if dst is None else dst, send_sem=send_sem, recv_sem=recv_sem,
            device_id=to, device_id_type=MESH,
        )
        copy.start()
        pending.append(copy)

    def arrived(ref, sem):
        pltpu.make_async_copy(ref, ref, sem).wait()

    def both_ways(ref, axis, send_sems, recv_sems):
        send(ref, send_sems(0), recv_sems(1), device(*moved(me, axis, 1)))
        send(ref, send_sems(1), recv_sems(2), device(*moved(me, axis, -1)))

    def to_sibling(p, k, ref):
        send(ref, sc.at[p, k], rc.at[p, k], sibling)

    for p, part in enumerate(PARTS):
        both_ways(block_at(w, me, part), part[2][0], lambda k: s1.at[p, k], lambda k: r1.at[p, k])
    for d in range(1, 8):
        peer = lax.rem(chan + d, 8)
        send(
            frames.at[:, pl.ds(pl.multiple_of(peer * 256, 256), 256)], fr_send.at[d - 1], fr_recv.at[d - 1],
            (tm, peer), mine.at[chan],
        )
    for p, part in enumerate(PARTS):
        both_ways(block_at(w, me, part), part[2][1], lambda k: s2.at[p, 0, k], lambda k: r2.at[p, 0, k])
    for p, part in enumerate(PARTS):
        both_ways(block_at(w, me, part), part[2][2], lambda k: s0.at[p, 0, k], lambda k: r0.at[p, 0, k])
    for k in (1, 2, 3):
        for p, part in enumerate(PARTS):
            a, b, c = part[2]
            block = block_at(w, moved(me, a, STEPS[k]), part)
            arrived(block, r1.at[p, k])
            if k == 1 + p % 2:
                send(block, s1.at[p, 2], r1.at[p, 3], device(*moved(me, a, -STEPS[k])))
            both_ways(block, b, lambda q: s2.at[p, k, q], lambda q: r2.at[p, k, q])
            both_ways(block, c, lambda q: s0.at[p, k, q], lambda q: r0.at[p, k, q])
    for p, part in enumerate(PARTS):
        to_sibling(p, 0, column_at(w, me, part))

    def second(j):
        for p, part in enumerate(PARTS):
            a, b, c = part[2]
            for k in range(4):
                block = block_at(w, moved(moved(me, b, STEPS[j]), a, STEPS[k]), part)
                arrived(block, r2.at[p, k, j])
                if j == 1 + k % 2:
                    send(block, s2.at[p, k, 2], r2.at[p, k, 3], device(*moved(me, b, -STEPS[j])))
            column = column_at(w, moved(me, b, STEPS[j]), part)
            both_ways(column, c, lambda q: s3.at[p, j, q], lambda q: r3.at[p, j, q])
            to_sibling(p, j, column)

    def third(i, j, p):
        part = PARTS[p]
        a, b, c = part[2]
        at = moved(moved(me, c, STEPS[i]), b, STEPS[j])
        column = column_at(w, at, part)
        if j == 0 and i < 3:
            for k in range(4):
                arrived(block_at(w, moved(at, a, STEPS[k]), part), r0.at[p, k, i])
        else:
            arrived(column, r3.at[p, j, i])
        if i == 1 + j % 2:
            send(column, s3.at[p, j, 2], r3.at[p, j, 3], device(*moved(me, c, -STEPS[i])))
        to_sibling(p, 4 * i + j, column)

    other = (x, y, z, 1 - core)

    def from_sibling(i, j, p):
        _, b, c = PARTS[p][2]
        arrived(column_at(w, moved(moved(other, c, STEPS[i]), b, STEPS[j]), PARTS[p]), rc.at[p, 4 * i + j])

    second(1)
    for i in (1, 2):
        for p in range(3):
            third(i, 0, p)

    locals_[2].wait()
    for d in range(1, 8):
        arrived(mine.at[lax.rem(chan + 8 - d, 8)], fr_recv.at[d - 1])
    x_in[...] = jnp.transpose(mine[...].astype(jnp.float32).reshape(1280, 256))
    normed_in[...] = norm_rows(x_in[...], gain_row(ffn_gain)).astype(jnp.bfloat16)
    total[...] = jnp.zeros_like(total)

    second(2)
    second(3)
    for j in (1, 2, 3):
        for i in (1, 2):
            for p in range(3):
                third(i, j, p)

    def ffn(zz, xx):
        up_all = w[zz, xx, :, :, :, 0:80, :].reshape(1280, 640)
        down_all = w[zz, xx, :, :, :, 80:160, :].reshape(1280, 640)
        pre = jnp.dot(normed_in[...], up_all, preferred_element_type=jnp.float32)
        hidden = (pre / (1.0 + jnp.exp(-pre))).astype(jnp.bfloat16)
        total[...] += lax.dot_general(hidden, down_all, NT, preferred_element_type=jnp.float32)

    def ffn_loop(first, count, xx):
        def one(q, carry):
            ffn(lax.rem(z + q, 4), xx)
            return carry

        lax.fori_loop(first, first + count, one, 0)

    for j in (0, 1, 2):
        third(3, j, 0)
    for i in range(3):
        for j in range(4):
            for p in range(3):
                from_sibling(i, j, p)
    for j in (0, 1, 2):
        from_sibling(3, j, 0)
    ffn_loop(3, 3, x // 2)
    for j in range(4):
        third(3, j, 2)
    third(3, 3, 0)
    for j in range(4):
        third(3, j, 1)
    for j in range(4):
        from_sibling(3, j, 2)
    ffn_loop(2, 1, x // 2)
    from_sibling(3, 3, 0)
    for j in range(4):
        from_sibling(3, j, 1)
    ffn_loop(0, 4, 1 - x // 2)

    locals_[3].wait()
    residual = x_in[...] + 0.5 * total[...]
    normed = norm_rows(residual, gain_row(final_gain)).astype(jnp.bfloat16)
    logits = jnp.dot(normed, ctc[...], preferred_element_type=jnp.float32)
    shifted = logits - jnp.max(logits, axis=-1, keepdims=True)
    emis[...] = shifted - jnp.log(jnp.sum(jnp.exp(shifted), axis=-1, keepdims=True))
    for copy in pending:
        copy.wait_send()


def block_part(frames, up, down, ffn_gain, final_gain, ctc):
    dma = pltpu.SemaphoreType.DMA
    return pl.pallas_call(
        block_kernel,
        out_shape=jax.ShapeDtypeStruct((256, 256), jnp.float32),
        in_specs=[ANY, ANY, ANY, VM, VM, ANY],
        out_specs=VM,
        scratch_shapes=[
            pltpu.VMEM((4, 2, 2, 4, 2, 160, 640), jnp.bfloat16),
            pltpu.VMEM((8, 160, 256), jnp.bfloat16),
            pltpu.VMEM((1280, 256), jnp.bfloat16),
            pltpu.VMEM((256, 1280), jnp.float32),
            pltpu.VMEM((256, 1280), jnp.bfloat16),
            pltpu.VMEM((256, 1280), jnp.float32),
            dma((4,)), dma((7,)), dma((7,)),
            dma((3, 3)), dma((3, 4)),
            dma((3, 4, 3)), dma((3, 4, 4)),
            dma((3, 4, 2)), dma((3, 4, 3)),
            dma((3, 4, 3)), dma((3, 4, 4)),
            dma((3, 16)), dma((3, 16)),
        ],
        compiler_params=pltpu.CompilerParams(collective_id=1, has_side_effects=True, vmem_limit_bytes=52 * MIB),
        name="block",
    )(frames, up, down, ffn_gain, final_gain, ctc)


def split(values):
    high = values.astype(jnp.bfloat16)
    return high, (values - high.astype(jnp.float32)).astype(jnp.bfloat16)


def state_ids(labels, base):
    row0 = jnp.minimum(base // 128, 61)
    window = jnp.concatenate([labels[pl.ds(row0 + k, 1), :] for k in range(3)], axis=1)
    r = lax.broadcasted_iota(jnp.int32, (128, 384), 0)
    lane = lax.broadcasted_iota(jnp.int32, (128, 384), 1)
    at = base - row0 * 128 + 2 * ((r % 8) * 16 + r // 8) + 1
    pick = lambda here: jnp.sum(jnp.where(lane == here, window, 0), axis=1, keepdims=True)
    return pick(at), pick(at - 2)


def transfer_matrix(emissions, labels, start_in, width_in, start_out, width_out, states):
    par = lax.rem(start_in, 2)
    offset = start_out - start_in
    ids, ids_before = state_ids(labels, start_in - par)
    char = lax.broadcasted_iota(jnp.int32, (128, 256), 1)
    choose = ((ids == char).astype(jnp.float32) - (char == 0).astype(jnp.float32)).astype(jnp.bfloat16)
    high, low = split(emissions)
    rest = (emissions - high.astype(jnp.float32) - low.astype(jnp.float32)).astype(jnp.bfloat16)
    gain = sum(lax.dot_general(choose, part, NT, preferred_element_type=jnp.float32) for part in (high, low, rest))
    blank = jnp.sum(emissions[:, 0:1])
    skip = jnp.broadcast_to(jnp.where(ids == ids_before, NEG, 0.0), (128, 128)).reshape(16, 8, 128)
    v = lax.broadcasted_iota(jnp.int32, (16, 8, 128), 0)
    sub = lax.broadcasted_iota(jnp.int32, (16, 8, 128), 1)
    start = lax.broadcasted_iota(jnp.int32, (16, 8, 128), 2)
    at = 2 * (sub * 16 + v) - par
    live = start < width_in
    even = jnp.where((at == start) & live, 0.0, NEG)
    odd = jnp.where((at + 1 == start) & live, 0.0, NEG)
    top = jnp.full((8, 128), NEG, jnp.float32)
    first = lax.broadcasted_iota(jnp.int32, (8, 128), 0) == 0
    for half in range(2):
        block = gain[:, half * 128 : half * 128 + 128].reshape(16, 8, 128)
        for t in range(128):
            step = jnp.broadcast_to(block[:, :, t : t + 1], (16, 8, 128))
            turned = pltpu.roll(odd[15], 1, 0)
            below = jnp.concatenate([jnp.where(first, NEG, turned)[None], odd[:15]], axis=0)
            top = jnp.maximum(top, turned)
            odd = jnp.maximum(jnp.maximum(odd, even), below + skip) + step
            even = jnp.maximum(even, below)
    for k in range(16):
        states[pl.ds(2 * k, 8, stride=32), :] = even[k]
        states[pl.ds(2 * k + 1, 8, stride=32), :] = odd[k]
    states[256:264, :] = top
    reached = states[pl.ds(par + offset, 128), :]
    row = lax.broadcasted_iota(jnp.int32, (128, 128), 0)
    reached = jnp.where(row < width_out, reached + blank, NEG)
    return jnp.transpose(reached)


def row_to_column(row):
    i = lax.broadcasted_iota(jnp.int32, (128, 128), 0)
    j = lax.broadcasted_iota(jnp.int32, (128, 128), 1)
    return jnp.max(jnp.where(i == j, jnp.broadcast_to(row, (128, 128)), 4 * NEG), axis=1, keepdims=True)


def advance(column, matrix):
    return jnp.max(column + matrix, axis=0, keepdims=True)


def path_kernel(
    starts, widths, labels, emissions, out, states, transfer, group, rows, spans, entry, entries,
    ts, tr, ps, pr, es, er,
):
    tm, chan = lax.axis_index("tm"), lax.axis_index("chan")
    root = tm == 0
    barrier = pltpu.get_barrier_semaphore()
    for d in range(1, 8):
        pl.semaphore_signal(barrier, inc=1, device_id=(tm, lax.rem(chan + d, 8)), device_id_type=MESH)

    @pl.when(root)
    def _():
        def greet(g, carry):
            for d in range(8):

                @pl.when(jnp.logical_or(g != 0, d != 0))
                def _():
                    pl.semaphore_signal(barrier, inc=1, device_id=(g, lax.rem(chan + d, 8)), device_id_type=MESH)

            return carry

        lax.fori_loop(0, 16, greet, 0)

    @pl.when(jnp.logical_not(root))
    def _():
        pl.semaphore_signal(barrier, inc=1, device_id=(0, chan), device_id_type=MESH)

    shard = tm * 8 + chan
    prior = jnp.maximum(shard - 1, 0)
    start_in = jnp.where(shard > 0, starts[prior], 0)
    width_in = jnp.where(shard > 0, widths[prior], 2)
    transfer[...] = transfer_matrix(
        emissions[...], labels, start_in, width_in, starts[shard], widths[shard], states
    )

    @pl.when(root)
    def _():
        pl.semaphore_wait(barrier, 7 + 7 + 15)

    @pl.when(jnp.logical_not(root))
    def _():
        pl.semaphore_wait(barrier, 7 + 8)

    copies = []
    for d in range(1, 8):
        copy = pltpu.make_async_remote_copy(
            src_ref=transfer, dst_ref=group.at[chan], send_sem=ts.at[d - 1], recv_sem=tr.at[d - 1],
            device_id=(tm, lax.rem(chan + d, 8)), device_id_type=MESH,
        )
        copy.start()
        copies.append(copy)
    group[chan] = transfer[...]
    for copy in copies:
        copy.wait_recv()

    span = group[0, pl.ds(pl.multiple_of(chan * 16, 16), 16), :]

    def grow(m, span):
        best = span[:, 0:1] + group[m, 0:1, :]
        for i in range(1, 128):
            best = jnp.maximum(best, span[:, i : i + 1] + group[m, i : i + 1, :])
        return best

    rows[...] = lax.fori_loop(1, 8, grow, span)
    for copy in copies:
        copy.wait_send()

    at = pl.ds(pl.multiple_of(tm * 128 + chan * 16, 16), 16)
    for c in range(8):

        @pl.when(jnp.logical_not(jnp.logical_and(root, chan == c)))
        def _():
            pltpu.make_async_remote_copy(
                src_ref=rows, dst_ref=spans.at[at], send_sem=ps.at[c], recv_sem=pr,
                device_id=(0, c), device_id_type=MESH,
            ).start()

    @pl.when(root)
    def _():
        spans[at, :] = rows[...]
        row = jnp.zeros((1, 128), jnp.float32)
        entry[...] = jnp.broadcast_to(row, (8, 128))
        others = spans.at[pl.ds(0, 127 * 16)]
        pltpu.make_async_copy(others, others, pr).wait()

        def chain(g, row):
            row = advance(row_to_column(row), spans[pl.ds(pl.multiple_of(g * 128, 128), 128), :])
            entries[g] = jnp.broadcast_to(row, (8, 128))
            pltpu.make_async_remote_copy(
                src_ref=entries.at[g], dst_ref=entry, send_sem=es.at[g], recv_sem=er,
                device_id=(g + 1, chan), device_id_type=MESH,
            ).start()
            return row

        lax.fori_loop(0, 15, chain, row)

    @pl.when(jnp.logical_not(root))
    def _():
        pltpu.make_async_copy(entry, entry, er).wait()

    row = lax.fori_loop(0, chan + 1, lambda m, row: advance(row_to_column(row), group[m]), entry[0:1, :])
    out[...] = jnp.where(row > 0.5 * NEG, row * (1.0 / 32768), 0.0)

    @pl.when(root)
    def _():
        def sent(g, carry):
            pltpu.make_async_copy(entries.at[g], entries.at[g], es.at[g]).wait()
            return carry

        lax.fori_loop(0, 15, sent, 0)

    for c in range(8):

        @pl.when(jnp.logical_not(jnp.logical_and(root, chan == c)))
        def _():
            pltpu.make_async_copy(rows, rows, ps.at[c]).wait()


def path_part(starts, widths, labels, emissions):
    dma = pltpu.SemaphoreType.DMA
    smem = pl.BlockSpec(memory_space=pltpu.SMEM)
    return pl.pallas_call(
        path_kernel,
        out_shape=jax.ShapeDtypeStruct((1, 128), jnp.float32),
        in_specs=[smem, smem, VM, VM],
        out_specs=VM,
        scratch_shapes=[
            pltpu.VMEM((264, 128), jnp.float32),
            pltpu.VMEM((128, 128), jnp.float32),
            pltpu.VMEM((8, 128, 128), jnp.float32),
            pltpu.VMEM((16, 128), jnp.float32),
            pltpu.VMEM((2048, 128), jnp.float32),
            pltpu.VMEM((8, 128), jnp.float32),
            pltpu.VMEM((16, 8, 128), jnp.float32),
            dma((7,)), dma((7,)), dma((8,)), dma, dma((16,)), dma,
        ],
        compiler_params=pltpu.CompilerParams(collective_id=2, has_side_effects=True, vmem_limit_bytes=24 * MIB),
        name="path",
    )(starts, widths, labels, emissions)


def local(frames, up_weight, down_weight, ffn_gain, final_gain, ctc_weight, labels, starts, widths):
    emissions = block_part(
        frames.T, up_weight, down_weight.T, ffn_gain.reshape(10, 128), final_gain.reshape(10, 128), ctc_weight
    )
    return emissions, path_part(starts, widths, labels.reshape(64, 128), emissions)


def solution(mesh):
    in_specs = (P("tm", "chan"), P("tm", "chan"), P("chan", "tm"), P(), P(), P(), P(), P(), P())
    out_specs = (P(("tm", "chan"), None), P(("tm", "chan"), None))
    return jax.shard_map(local, mesh=mesh, in_specs=in_specs, out_specs=out_specs, check_vma=False)
```

time: 157 us -> 127 us (0.81)
  Pallas kernels: 140 us -> 119 us
  local copies, waits for them, and re-layouts: 10.6 us -> 6.57 us
  other arithmetic: 2.45 us -> 0 us
  between operations: 2.55 us -> 0.69 us
    pallas_call x3 -> x2, Pallas kernels: 140 us -> 119 us  [the longest x1 84.8 us: block_part(): pl.pallas_call(block_kernel, out_shape=jax.ShapeDtypeStruct((256, 256), j...]
    dynamic_slice x2 -> x0, local copies, waits for them, and re-layouts: 2.12 us -> none  [the longest x1 1.36 us: window_facts(): width_in = jnp.where(shard > 0, widths[prior], 2)]
    concatenate x2 -> x0, other arithmetic: 1.72 us -> none  [the longest x1 1.64 us: local(): chunk = jnp.concatenate([up_weight, down_weight.T], axis=0)]
    unnamed x8 -> x20, local copies, waits for them, and re-layouts: 6.26 us -> 6.57 us
where the time goes in v2:
time: 127 us; the launch traced here: 126 us
  Pallas kernels  119 us (94%)
  local copies, waits for them, and re-layouts  6.57 us (5%)
    pallas_call x1, Pallas kernels, block_part(): pl.pallas_call(block_kernel, out_shape=jax.ShapeDtypeStruct((256, 256), j...  84.8 us
    pallas_call x1, Pallas kernels, path_part(): pl.pallas_call(path_kernel, out_shape=jax.ShapeDtypeStruct((1, 128), jnp....  34.3 us
    unnamed x20, local copies, waits for them, and re-layouts  6.57 us

profile of v2, /device:TPU:27, one launch (start us, length us, event | category | flops | bytes accessed | tf_op | source)
XLA Modules:
  0.0 126.3 jit_solution(8633829171246340311)
XLA Ops:
  0.6 0.0 copy-start.5
  0.6 0.7 copy-done.5
  1.3 0.0 copy-start
  1.3 1.1 copy-done
  2.4 0.0 copy-start.1
  2.4 1.1 copy-done.1
  3.5 0.0 copy-start.2
  3.5 0.9 copy-done.2
  4.4 0.0 copy-start.3
  4.4 0.9 copy-done.3
  5.3 0.0 copy-start.6
  5.3 0.7 copy-done.6
  6.0 0.0 copy-start.4
  6.0 0.0 copy-start.7
  6.0 0.0 copy-start.8
  6.0 84.8 %block.1.emissions = f32[256,256]{1,0:T(8,128)S(1)} custom-call(bf16[160,2048]{1,0:T(8,128)(2,1)S(1)} %bitcast.5, bf16[80,640]{1,0:T(8,128)(2,1)S(1)} %copy-done.2, bf16[80,640]{1,0:T(8,128)(2,1)S(1)} %bitcast.6, f32[10,128]{1,0:T(8,128)S(1)} %bitcast.8, f32[10,128]{1,0:T(8,128)S(1)} %bitcast.9, bf16[1280,256]{1,0:T(8,128)(2,1)S(1)} %copy-done.1), custom_call_target="tpu_custom_call" | custom-call | tf_op jit(solution)/shard_map/block/pallas_call | solution.py:240
  90.8 0.0 copy-done.4
  90.8 0.0 copy-done.7
  90.8 0.0 copy-done.8
  90.8 34.3 %path.1 = f32[1,128]{1,0:T(1,128)S(1)} custom-call(s32[128]{0:T(128)S(1)} %copy-done.7, s32[128]{0:T(128)S(1)} %copy-done.8, s32[64,128]{1,0:T(8,128)S(1)} %bitcast.7, f32[256,256]{1,0:T(8,128)S(1)} %block.1.emissions), custom_call_target="tpu_custom_call" | custom-call | tf_op jit(solution)/shard_map/path/pallas_call | solution.py:449
  125.1 0.7 copy.13
  125.8 0.5 copy.14
Async XLA Ops:
  0.6 0.7 copy-start.5
  1.3 1.1 copy-start
  2.4 1.1 copy-start.1
  3.5 0.9 copy-start.2
  4.4 0.9 copy-start.3
  5.3 0.7 copy-start.6
  6.0 84.8 %copy-start.4 = (s32[8192]{0:T(1024)S(1)}, s32[8192]{0:T(1024)}, u32[]{:S(2)}) copy-start(s32[8192]{0:T(1024)} %param.15) | copy-start | bytes 98308
  6.0 84.8 %copy-start.7 = (s32[128]{0:T(128)S(1)}, s32[128]{0:T(128)}, u32[]{:S(2)}) copy-start(s32[128]{0:T(128)} %starts.1) | copy-start | bytes 1540
  6.0 84.8 %copy-start.8 = (s32[128]{0:T(128)S(1)}, s32[128]{0:T(128)}, u32[]{:S(2)}) copy-start(s32[128]{0:T(128)} %widths.1) | copy-start | bytes 1540

commit v3 on v2

--- a/solution.py
+++ b/solution.py
@@ -12,6 +12,7 @@
 NEG = -1e30
 MESH = pl.DeviceIdType.MESH
 ANY = pl.BlockSpec(memory_space=pl.ANY)
+HBM = pl.BlockSpec(memory_space=pltpu.HBM)
 VM = pl.BlockSpec(memory_space=pltpu.VMEM)
 MIB = 2**20
 
@@ -32,7 +33,33 @@
     return tuple(out)
 
 
-PARTS = ((0, 64, (2, 0, 1)), (64, 48, (1, 2, 0)), (112, 48, (0, 1, 2)))
+PARTS = (
+    (0, 64, (2, 0, 1)), (64, 48, (1, 2, 0)), (112, 48, (0, 1, 2)),
+)
+ALL = (0, 1, 2)
+ORDER = (
+    (0, 0, 1), (0, 0, 2), (0, 1, 1), (0, 1, 2), (0, 2, 1), (0, 2, 2), (1, 0, 0, 1), (1, 0, 0, 2), (1, 1, 0, 1),
+    (1, 1, 0, 2), (1, 2, 0, 1), (1, 2, 0, 2), (7, 0, 1), (3, 0, 1), (1, 0, 1, 1), (1, 0, 1, 2), (7, 1, 1),
+    (1, 1, 1, 1), (1, 1, 1, 2), (7, 2, 1), (3, 2, 1), (1, 2, 1, 1), (1, 2, 1, 2), (7, 0, 2), (1, 0, 2, 1),
+    (1, 0, 2, 2), (7, 1, 2), (3, 1, 2), (1, 1, 2, 1), (1, 1, 2, 2), (7, 2, 2), (1, 2, 2, 1), (1, 2, 2, 2),
+    (7, 0, 3), (1, 0, 3, 1), (1, 0, 3, 2), (7, 1, 3), (1, 1, 3, 1), (1, 1, 3, 2), (7, 2, 3), (1, 2, 3, 1),
+    (1, 2, 3, 2), (2, 0, 0, 1), (2, 0, 0, 2), (2, 1, 0, 1), (2, 1, 0, 2), (2, 2, 0, 1), (2, 2, 0, 2), (8, 0, 0, 1),
+    (4, 0, 0, 1), (8, 0, 1, 1), (8, 0, 2, 1), (4, 0, 2, 1), (8, 0, 3, 1), (2, 0, 1, 1), (2, 0, 1, 2), (8, 1, 0, 1),
+    (4, 1, 0, 1), (8, 1, 1, 1), (8, 1, 2, 1), (4, 1, 2, 1), (8, 1, 3, 1), (2, 1, 1, 1), (2, 1, 1, 2), (8, 2, 0, 1),
+    (4, 2, 0, 1), (8, 2, 1, 1), (8, 2, 2, 1), (4, 2, 2, 1), (8, 2, 3, 1), (2, 2, 1, 1), (2, 2, 1, 2), (6,),
+    (8, 0, 0, 2), (8, 0, 1, 2), (4, 0, 1, 2), (8, 0, 2, 2), (8, 0, 3, 2), (4, 0, 3, 2), (2, 0, 2, 1), (2, 0, 2, 2),
+    (8, 1, 0, 2), (8, 1, 1, 2), (4, 1, 1, 2), (8, 1, 2, 2), (8, 1, 3, 2), (4, 1, 3, 2), (2, 1, 2, 1), (2, 1, 2, 2),
+    (8, 2, 0, 2), (8, 2, 1, 2), (4, 2, 1, 2), (8, 2, 2, 2), (8, 2, 3, 2), (4, 2, 3, 2), (2, 2, 2, 1), (2, 2, 2, 2),
+    (8, 0, 0, 3), (8, 0, 1, 3), (8, 0, 2, 3), (8, 0, 3, 3), (2, 0, 3, 1), (2, 0, 3, 2), (8, 1, 0, 3), (8, 1, 1, 3),
+    (8, 1, 2, 3), (8, 1, 3, 3), (2, 1, 3, 1), (2, 1, 3, 2), (8, 2, 0, 3), (8, 2, 1, 3), (8, 2, 2, 3), (8, 2, 3, 3),
+    (2, 2, 3, 1), (2, 2, 3, 2), (9, 0, 0, 1), (5, 0, 0, 1), (9, 1, 0, 1), (5, 1, 0, 1), (9, 2, 0, 1), (5, 2, 0, 1),
+    (9, 0, 1, 1), (9, 1, 1, 1), (9, 2, 1, 1), (9, 0, 2, 1), (5, 0, 2, 1), (9, 1, 2, 1), (5, 1, 2, 1), (9, 2, 2, 1),
+    (5, 2, 2, 1), (9, 0, 3, 1), (9, 1, 3, 1), (9, 2, 3, 1), (10,), (9, 0, 0, 2), (9, 1, 0, 2), (9, 2, 0, 2),
+    (9, 0, 1, 2), (5, 0, 1, 2), (9, 1, 1, 2), (5, 1, 1, 2), (9, 2, 1, 2), (5, 2, 1, 2), (9, 0, 2, 2), (9, 1, 2, 2),
+    (9, 2, 2, 2), (9, 0, 3, 2), (5, 0, 3, 2), (9, 1, 3, 2), (5, 1, 3, 2), (9, 2, 3, 2), (5, 2, 3, 2), (9, 0, 0, 3),
+    (9, 0, 1, 3), (9, 0, 2, 3), (9, 2, 0, 3), (9, 2, 1, 3), (9, 2, 2, 3), (9, 2, 3, 3), (9, 0, 3, 3), (9, 1, 0, 3),
+    (9, 1, 1, 3), (9, 1, 2, 3), (9, 1, 3, 3),
+)
 STEPS = (0, -1, 1, 2)
 NT = (((1,), (1,)), ((), ()))
 
@@ -53,6 +80,16 @@
     return w.at[:, x // 2, lax.rem(x, 2), y, core, pl.ds(row, rows)]
 
 
+def slab_at(w, pos, part):
+    x, y, z, core = pos
+    row, rows, (_, _, axis) = part
+    if axis == 0:
+        return w.at[:, x // 2, lax.rem(x, 2), :, core, pl.ds(row, rows)]
+    if axis == 1:
+        return w.at[:, :, :, y, core, pl.ds(row, rows)]
+    return w.at[z, :, :, :, core, pl.ds(row, rows)]
+
+
 def norm_rows(values, gain_row):
     row_mean = jnp.mean(values, axis=-1, keepdims=True)
     centred = values - row_mean
@@ -67,7 +104,7 @@
 def block_kernel(
     frames, up, down, ffn_gain, final_gain, ctc_hbm, emis,
     w, mine, ctc, x_in, normed_in, total,
-    local_sem, fr_send, fr_recv, s1, r1, s2, r2, s0, r0, s3, r3, sc, rc,
+    local_sem, fr_send, fr_recv, s1, r1, s2, r2, s3, r3, sc, rc,
 ):
     me = position()
     x, y, z, core = me
@@ -114,116 +151,120 @@
     def to_sibling(p, k, ref):
         send(ref, sc.at[p, k], rc.at[p, k], sibling)
 
-    for p, part in enumerate(PARTS):
-        both_ways(block_at(w, me, part), part[2][0], lambda k: s1.at[p, k], lambda k: r1.at[p, k])
-    for d in range(1, 8):
-        peer = lax.rem(chan + d, 8)
-        send(
-            frames.at[:, pl.ds(pl.multiple_of(peer * 256, 256), 256)], fr_send.at[d - 1], fr_recv.at[d - 1],
-            (tm, peer), mine.at[chan],
-        )
-    for p, part in enumerate(PARTS):
-        both_ways(block_at(w, me, part), part[2][1], lambda k: s2.at[p, 0, k], lambda k: r2.at[p, 0, k])
-    for p, part in enumerate(PARTS):
-        both_ways(block_at(w, me, part), part[2][2], lambda k: s0.at[p, 0, k], lambda k: r0.at[p, 0, k])
-    for k in (1, 2, 3):
-        for p, part in enumerate(PARTS):
-            a, b, c = part[2]
-            block = block_at(w, moved(me, a, STEPS[k]), part)
-            arrived(block, r1.at[p, k])
-            if k == 1 + p % 2:
-                send(block, s1.at[p, 2], r1.at[p, 3], device(*moved(me, a, -STEPS[k])))
-            both_ways(block, b, lambda q: s2.at[p, k, q], lambda q: r2.at[p, k, q])
-            both_ways(block, c, lambda q: s0.at[p, k, q], lambda q: r0.at[p, k, q])
-    for p, part in enumerate(PARTS):
-        to_sibling(p, 0, column_at(w, me, part))
-
-    def second(j):
-        for p, part in enumerate(PARTS):
-            a, b, c = part[2]
-            for k in range(4):
-                block = block_at(w, moved(moved(me, b, STEPS[j]), a, STEPS[k]), part)
-                arrived(block, r2.at[p, k, j])
-                if j == 1 + k % 2:
-                    send(block, s2.at[p, k, 2], r2.at[p, k, 3], device(*moved(me, b, -STEPS[j])))
-            column = column_at(w, moved(me, b, STEPS[j]), part)
-            both_ways(column, c, lambda q: s3.at[p, j, q], lambda q: r3.at[p, j, q])
-            to_sibling(p, j, column)
-
-    def third(i, j, p):
+    def step_to(pos, axis, place):
+        return moved(pos, axis, STEPS[place])
+
+    def send_to(ref, axis, q, send_sem, recv_sem):
+        send(ref, send_sem, recv_sem, device(*moved(me, axis, 1 if q == 1 else -1)))
+
+    arrivals = {}
+
+    def count(key, full):
+        arrivals[key] = arrivals.get(key, 0) + 1
+        return arrivals[key] == full
+
+    def communicate(event):
+        kind, p, *at = event
         part = PARTS[p]
         a, b, c = part[2]
-        at = moved(moved(me, c, STEPS[i]), b, STEPS[j])
-        column = column_at(w, at, part)
-        if j == 0 and i < 3:
-            for k in range(4):
-                arrived(block_at(w, moved(at, a, STEPS[k]), part), r0.at[p, k, i])
+        if kind == 0:
+            (q,) = at
+            send_to(block_at(w, me, part), a, q, s1.at[p, q - 1], r1.at[p, q])
+        elif kind == 1:
+            k, q = at
+            send_to(block_at(w, step_to(me, a, k), part), b, q, s2.at[p, k, q - 1], r2.at[p, k, q])
+        elif kind == 2:
+            j, q = at
+            send_to(column_at(w, step_to(me, b, j), part), c, q, s3.at[p, j, q - 1], r3.at[p, j, q])
+        elif kind == 3:
+            (k,) = at
+            send_to(block_at(w, step_to(me, a, k), part), a, k, s1.at[p, 2], r1.at[p, 3])
+        elif kind == 4:
+            k, j = at
+            send_to(block_at(w, step_to(step_to(me, b, j), a, k), part), b, j, s2.at[p, k, 2], r2.at[p, k, 3])
+        elif kind == 5:
+            j, i = at
+            send_to(column_at(w, step_to(step_to(me, c, i), b, j), part), c, i, s3.at[p, j, 2], r3.at[p, j, 3])
+        elif kind == 7:
+            (k,) = at
+            arrived(block_at(w, step_to(me, a, k), part), r1.at[p, k])
+            if count((p, 0), 15):
+                to_sibling(p, 0, slab_at(w, me, part))
+        elif kind == 8:
+            k, j = at
+            arrived(block_at(w, step_to(step_to(me, b, j), a, k), part), r2.at[p, k, j])
+            if count((p, 0), 15):
+                to_sibling(p, 0, slab_at(w, me, part))
+        elif kind == 9:
+            j, i = at
+            there = step_to(step_to(me, c, i), b, j)
+            column = column_at(w, there, part)
+            arrived(column, r3.at[p, j, i])
+            if i == 3:
+                to_sibling(p, 3 + j, column)
+            elif count((p, i), 4):
+                to_sibling(p, i, slab_at(w, there, part))
+
+    other = (x, y, z, 1 - core)
+
+    def slab_from_sibling(i, p):
+        c = PARTS[p][2][2]
+        arrived(slab_at(w, moved(other, c, STEPS[i]), PARTS[p]), rc.at[p, i])
+
+    def from_sibling(j, p):
+        _, b, c = PARTS[p][2]
+        arrived(column_at(w, moved(moved(other, c, 2), b, STEPS[j]), PARTS[p]), rc.at[p, 3 + j])
+
+    def send_frames():
+        for d in range(1, 8):
+            peer = lax.rem(chan + d, 8)
+            send(
+                frames.at[:, pl.ds(pl.multiple_of(peer * 256, 256), 256)], fr_send.at[d - 1], fr_recv.at[d - 1],
+                (tm, peer), mine.at[chan],
+            )
+
+    def norm_frames():
+        locals_[2].wait()
+        for d in range(1, 8):
+            arrived(mine.at[lax.rem(chan + 8 - d, 8)], fr_recv.at[d - 1])
+        x_in[...] = jnp.transpose(mine[...].astype(jnp.float32).reshape(1280, 256))
+        normed_in[...] = norm_rows(x_in[...], gain_row(ffn_gain)).astype(jnp.bfloat16)
+        total[...] = jnp.zeros_like(total)
+
+    def project(first_step, count, xx):
+        def one(q, carry):
+            zz = lax.rem(z + q, 4)
+            up_all = w[zz, xx, :, :, :, 0:80, :].reshape(1280, 640)
+            down_all = w[zz, xx, :, :, :, 80:160, :].reshape(1280, 640)
+            pre = jnp.dot(normed_in[...], up_all, preferred_element_type=jnp.float32)
+            half = 0.5 * pre
+            hidden = (half + half * jnp.tanh(half)).astype(jnp.bfloat16)
+            total[...] += lax.dot_general(hidden, down_all, NT, preferred_element_type=jnp.float32)
+            return carry
+
+        lax.fori_loop(first_step, first_step + count, one, 0)
+
+    for event in ORDER:
+        if event[0] == 6:
+            send_frames()
+        elif event[0] == 10:
+            norm_frames()
         else:
-            arrived(column, r3.at[p, j, i])
-        if i == 1 + j % 2:
-            send(column, s3.at[p, j, 2], r3.at[p, j, 3], device(*moved(me, c, -STEPS[i])))
-        to_sibling(p, 4 * i + j, column)
-
-    other = (x, y, z, 1 - core)
-
-    def from_sibling(i, j, p):
-        _, b, c = PARTS[p][2]
-        arrived(column_at(w, moved(moved(other, c, STEPS[i]), b, STEPS[j]), PARTS[p]), rc.at[p, 4 * i + j])
-
-    second(1)
-    for i in (1, 2):
-        for p in range(3):
-            third(i, 0, p)
-
-    locals_[2].wait()
-    for d in range(1, 8):
-        arrived(mine.at[lax.rem(chan + 8 - d, 8)], fr_recv.at[d - 1])
-    x_in[...] = jnp.transpose(mine[...].astype(jnp.float32).reshape(1280, 256))
-    normed_in[...] = norm_rows(x_in[...], gain_row(ffn_gain)).astype(jnp.bfloat16)
-    total[...] = jnp.zeros_like(total)
-
-    second(2)
-    second(3)
-    for j in (1, 2, 3):
-        for i in (1, 2):
-            for p in range(3):
-                third(i, j, p)
-
-    def ffn(zz, xx):
-        up_all = w[zz, xx, :, :, :, 0:80, :].reshape(1280, 640)
-        down_all = w[zz, xx, :, :, :, 80:160, :].reshape(1280, 640)
-        pre = jnp.dot(normed_in[...], up_all, preferred_element_type=jnp.float32)
-        hidden = (pre / (1.0 + jnp.exp(-pre))).astype(jnp.bfloat16)
-        total[...] += lax.dot_general(hidden, down_all, NT, preferred_element_type=jnp.float32)
-
-    def ffn_loop(first, count, xx):
-        def one(q, carry):
-            ffn(lax.rem(z + q, 4), xx)
-            return carry
-
-        lax.fori_loop(first, first + count, one, 0)
-
+            communicate(event)
+    on_y, on_x, on_z = ALL
+    for p in ALL:
+        for i in range(3):
+            slab_from_sibling(i, p)
     for j in (0, 1, 2):
-        third(3, j, 0)
-    for i in range(3):
-        for j in range(4):
-            for p in range(3):
-                from_sibling(i, j, p)
-    for j in (0, 1, 2):
-        from_sibling(3, j, 0)
-    ffn_loop(3, 3, x // 2)
+        from_sibling(j, on_y)
+    project(3, 3, x // 2)
     for j in range(4):
-        third(3, j, 2)
-    third(3, 3, 0)
+        from_sibling(j, on_z)
+    project(2, 1, x // 2)
+    from_sibling(3, on_y)
     for j in range(4):
-        third(3, j, 1)
-    for j in range(4):
-        from_sibling(3, j, 2)
-    ffn_loop(2, 1, x // 2)
-    from_sibling(3, 3, 0)
-    for j in range(4):
-        from_sibling(3, j, 1)
-    ffn_loop(0, 4, 1 - x // 2)
+        from_sibling(j, on_x)
+    project(0, 4, 1 - x // 2)
 
     locals_[3].wait()
     residual = x_in[...] + 0.5 * total[...]
@@ -240,7 +281,7 @@
     return pl.pallas_call(
         block_kernel,
         out_shape=jax.ShapeDtypeStruct((256, 256), jnp.float32),
-        in_specs=[ANY, ANY, ANY, VM, VM, ANY],
+        in_specs=[HBM, HBM, HBM, VM, VM, HBM],
         out_specs=VM,
         scratch_shapes=[
             pltpu.VMEM((4, 2, 2, 4, 2, 160, 640), jnp.bfloat16),
@@ -252,9 +293,8 @@
             dma((4,)), dma((7,)), dma((7,)),
             dma((3, 3)), dma((3, 4)),
             dma((3, 4, 3)), dma((3, 4, 4)),
-            dma((3, 4, 2)), dma((3, 4, 3)),
             dma((3, 4, 3)), dma((3, 4, 4)),
-            dma((3, 16)), dma((3, 16)),
+            dma((3, 7)), dma((3, 7)),
         ],
         compiler_params=pltpu.CompilerParams(collective_id=1, has_side_effects=True, vmem_limit_bytes=52 * MIB),
         name="block",

time: 127 us -> 116 us (0.913)
  Pallas kernels: 119 us -> 109 us
    pallas_call x1, Pallas kernels: 84.8 us -> 76 us  [block_part(): pl.pallas_call(block_kernel, out_shape=jax.ShapeDtypeStruct((256, 256), j...]
    pallas_call x1, Pallas kernels: 34.3 us -> 32.5 us  [path_part(): pl.pallas_call(path_kernel, out_shape=jax.ShapeDtypeStruct((1, 128), jnp....]
where the time goes in v3:
time: 116 us
  Pallas kernels  109 us (94%)
  local copies, waits for them, and re-layouts  6.57 us (6%)
    pallas_call x1, Pallas kernels, block_part(): pl.pallas_call(block_kernel, out_shape=jax.ShapeDtypeStruct((256, 256), j...  76 us
    pallas_call x1, Pallas kernels, path_part(): pl.pallas_call(path_kernel, out_shape=jax.ShapeDtypeStruct((1, 128), jnp....  32.5 us
    unnamed x20, local copies, waits for them, and re-layouts  6.57 us

profile of v3, /device:TPU:27, one launch (start us, length us, event | category | flops | bytes accessed | tf_op | source)
XLA Modules:
  0.0 115.8 jit_solution(1557427383851633543)
XLA Ops:
  0.6 0.0 copy-start.5
  0.6 0.7 copy-done.5
  1.3 0.0 copy-start
  1.3 1.1 copy-done
  2.4 0.0 copy-start.1
  2.4 1.1 copy-done.1
  3.5 0.0 copy-start.2
  3.5 0.9 copy-done.2
  4.4 0.0 copy-start.3
  4.4 0.9 copy-done.3
  5.3 0.0 copy-start.6
  5.3 0.7 copy-done.6
  6.0 0.0 copy-start.4
  6.0 0.0 copy-start.7
  6.0 0.0 copy-start.8
  6.0 76.0 %block.1.emissions = f32[256,256]{1,0:T(8,128)S(1)} custom-call(bf16[160,2048]{1,0:T(8,128)(2,1)S(1)} %bitcast.5, bf16[80,640]{1,0:T(8,128)(2,1)S(1)} %copy-done.2, bf16[80,640]{1,0:T(8,128)(2,1)S(1)} %bitcast.6, f32[10,128]{1,0:T(8,128)S(1)} %bitcast.8, f32[10,128]{1,0:T(8,128)S(1)} %bitcast.9, bf16[1280,256]{1,0:T(8,128)(2,1)S(1)} %copy-done.1), custom_call_target="tpu_custom_call" | custom-call | tf_op jit(solution)/shard_map/block/pallas_call | solution.py:281
  82.0 0.0 copy-done.4
  82.0 0.0 copy-done.7
  82.1 0.0 copy-done.8
  82.1 32.5 %path.1 = f32[1,128]{1,0:T(1,128)S(1)} custom-call(s32[128]{0:T(128)S(1)} %copy-done.7, s32[128]{0:T(128)S(1)} %copy-done.8, s32[64,128]{1,0:T(8,128)S(1)} %bitcast.7, f32[256,256]{1,0:T(8,128)S(1)} %block.1.emissions), custom_call_target="tpu_custom_call" | custom-call | tf_op jit(solution)/shard_map/path/pallas_call | solution.py:489
  114.5 0.7 copy.13
  115.3 0.5 copy.14
Async XLA Ops:
  0.6 0.7 copy-start.5
  1.3 1.1 copy-start
  2.4 1.1 copy-start.1
  3.5 0.9 copy-start.2
  4.4 0.9 copy-start.3
  5.3 0.7 copy-start.6
  6.0 76.0 %copy-start.4 = (s32[8192]{0:T(1024)S(1)}, s32[8192]{0:T(1024)}, u32[]{:S(2)}) copy-start(s32[8192]{0:T(1024)} %param.15) | copy-start | bytes 98308
  6.0 76.1 %copy-start.7 = (s32[128]{0:T(128)S(1)}, s32[128]{0:T(128)}, u32[]{:S(2)}) copy-start(s32[128]{0:T(128)} %starts.1) | copy-start | bytes 1540
  6.0 76.1 %copy-start.8 = (s32[128]{0:T(128)S(1)}, s32[128]{0:T(128)}, u32[]{:S(2)}) copy-start(s32[128]{0:T(128)} %widths.1) | copy-start | bytes 1540

commit v4 on v3

--- a/solution.py
+++ b/solution.py
@@ -38,27 +38,27 @@
 )
 ALL = (0, 1, 2)
 ORDER = (
-    (0, 0, 1), (0, 0, 2), (0, 1, 1), (0, 1, 2), (0, 2, 1), (0, 2, 2), (1, 0, 0, 1), (1, 0, 0, 2), (1, 1, 0, 1),
-    (1, 1, 0, 2), (1, 2, 0, 1), (1, 2, 0, 2), (7, 0, 1), (3, 0, 1), (1, 0, 1, 1), (1, 0, 1, 2), (7, 1, 1),
-    (1, 1, 1, 1), (1, 1, 1, 2), (7, 2, 1), (3, 2, 1), (1, 2, 1, 1), (1, 2, 1, 2), (7, 0, 2), (1, 0, 2, 1),
-    (1, 0, 2, 2), (7, 1, 2), (3, 1, 2), (1, 1, 2, 1), (1, 1, 2, 2), (7, 2, 2), (1, 2, 2, 1), (1, 2, 2, 2),
-    (7, 0, 3), (1, 0, 3, 1), (1, 0, 3, 2), (7, 1, 3), (1, 1, 3, 1), (1, 1, 3, 2), (7, 2, 3), (1, 2, 3, 1),
-    (1, 2, 3, 2), (2, 0, 0, 1), (2, 0, 0, 2), (2, 1, 0, 1), (2, 1, 0, 2), (2, 2, 0, 1), (2, 2, 0, 2), (8, 0, 0, 1),
-    (4, 0, 0, 1), (8, 0, 1, 1), (8, 0, 2, 1), (4, 0, 2, 1), (8, 0, 3, 1), (2, 0, 1, 1), (2, 0, 1, 2), (8, 1, 0, 1),
-    (4, 1, 0, 1), (8, 1, 1, 1), (8, 1, 2, 1), (4, 1, 2, 1), (8, 1, 3, 1), (2, 1, 1, 1), (2, 1, 1, 2), (8, 2, 0, 1),
-    (4, 2, 0, 1), (8, 2, 1, 1), (8, 2, 2, 1), (4, 2, 2, 1), (8, 2, 3, 1), (2, 2, 1, 1), (2, 2, 1, 2), (6,),
-    (8, 0, 0, 2), (8, 0, 1, 2), (4, 0, 1, 2), (8, 0, 2, 2), (8, 0, 3, 2), (4, 0, 3, 2), (2, 0, 2, 1), (2, 0, 2, 2),
-    (8, 1, 0, 2), (8, 1, 1, 2), (4, 1, 1, 2), (8, 1, 2, 2), (8, 1, 3, 2), (4, 1, 3, 2), (2, 1, 2, 1), (2, 1, 2, 2),
-    (8, 2, 0, 2), (8, 2, 1, 2), (4, 2, 1, 2), (8, 2, 2, 2), (8, 2, 3, 2), (4, 2, 3, 2), (2, 2, 2, 1), (2, 2, 2, 2),
-    (8, 0, 0, 3), (8, 0, 1, 3), (8, 0, 2, 3), (8, 0, 3, 3), (2, 0, 3, 1), (2, 0, 3, 2), (8, 1, 0, 3), (8, 1, 1, 3),
-    (8, 1, 2, 3), (8, 1, 3, 3), (2, 1, 3, 1), (2, 1, 3, 2), (8, 2, 0, 3), (8, 2, 1, 3), (8, 2, 2, 3), (8, 2, 3, 3),
-    (2, 2, 3, 1), (2, 2, 3, 2), (9, 0, 0, 1), (5, 0, 0, 1), (9, 1, 0, 1), (5, 1, 0, 1), (9, 2, 0, 1), (5, 2, 0, 1),
-    (9, 0, 1, 1), (9, 1, 1, 1), (9, 2, 1, 1), (9, 0, 2, 1), (5, 0, 2, 1), (9, 1, 2, 1), (5, 1, 2, 1), (9, 2, 2, 1),
-    (5, 2, 2, 1), (9, 0, 3, 1), (9, 1, 3, 1), (9, 2, 3, 1), (10,), (9, 0, 0, 2), (9, 1, 0, 2), (9, 2, 0, 2),
-    (9, 0, 1, 2), (5, 0, 1, 2), (9, 1, 1, 2), (5, 1, 1, 2), (9, 2, 1, 2), (5, 2, 1, 2), (9, 0, 2, 2), (9, 1, 2, 2),
-    (9, 2, 2, 2), (9, 0, 3, 2), (5, 0, 3, 2), (9, 1, 3, 2), (5, 1, 3, 2), (9, 2, 3, 2), (5, 2, 3, 2), (9, 0, 0, 3),
-    (9, 0, 1, 3), (9, 0, 2, 3), (9, 2, 0, 3), (9, 2, 1, 3), (9, 2, 2, 3), (9, 2, 3, 3), (9, 0, 3, 3), (9, 1, 0, 3),
-    (9, 1, 1, 3), (9, 1, 2, 3), (9, 1, 3, 3),
+    (0, 0, 1), (0, 0, 2), (0, 0, 3), (0, 1, 1), (0, 1, 2), (0, 1, 3), (0, 2, 1), (0, 2, 2), (0, 2, 3), (1, 0, 0, 1),
+    (1, 0, 0, 2), (1, 1, 0, 1), (1, 1, 0, 2), (1, 2, 0, 1), (1, 2, 0, 2), (7, 0, 1), (1, 0, 1, 1), (1, 0, 1, 2),
+    (7, 1, 1), (1, 1, 1, 1), (1, 1, 1, 2), (7, 2, 1), (1, 2, 1, 1), (1, 2, 1, 2), (7, 0, 2), (1, 0, 2, 1),
+    (1, 0, 2, 2), (7, 1, 2), (1, 1, 2, 1), (1, 1, 2, 2), (7, 2, 2), (1, 2, 2, 1), (1, 2, 2, 2), (7, 0, 3),
+    (1, 0, 3, 1), (1, 0, 3, 2), (7, 1, 3), (1, 1, 3, 1), (1, 1, 3, 2), (7, 2, 3), (1, 2, 3, 1), (1, 2, 3, 2),
+    (2, 0, 0, 1), (2, 0, 0, 2), (2, 1, 0, 1), (2, 1, 0, 2), (2, 2, 0, 1), (2, 2, 0, 2), (8, 0, 0, 1), (4, 0, 0, 1),
+    (8, 0, 1, 1), (8, 0, 2, 1), (4, 0, 2, 1), (8, 0, 3, 1), (2, 0, 1, 1), (2, 0, 1, 2), (8, 1, 0, 1), (4, 1, 0, 1),
+    (8, 1, 1, 1), (8, 1, 2, 1), (4, 1, 2, 1), (8, 1, 3, 1), (2, 1, 1, 1), (2, 1, 1, 2), (8, 2, 0, 1), (4, 2, 0, 1),
+    (8, 2, 1, 1), (8, 2, 2, 1), (4, 2, 2, 1), (8, 2, 3, 1), (2, 2, 1, 1), (2, 2, 1, 2), (6,), (8, 0, 0, 2),
+    (8, 0, 1, 2), (4, 0, 1, 2), (8, 0, 2, 2), (8, 0, 3, 2), (4, 0, 3, 2), (2, 0, 2, 1), (2, 0, 2, 2), (8, 1, 0, 2),
+    (8, 1, 1, 2), (4, 1, 1, 2), (8, 1, 2, 2), (8, 1, 3, 2), (4, 1, 3, 2), (2, 1, 2, 1), (2, 1, 2, 2), (8, 2, 0, 2),
+    (8, 2, 1, 2), (4, 2, 1, 2), (8, 2, 2, 2), (8, 2, 3, 2), (4, 2, 3, 2), (2, 2, 2, 1), (2, 2, 2, 2), (8, 0, 0, 3),
+    (8, 0, 1, 3), (8, 0, 2, 3), (8, 0, 3, 3), (2, 0, 3, 1), (2, 0, 3, 2), (8, 1, 0, 3), (8, 1, 1, 3), (8, 1, 2, 3),
+    (8, 1, 3, 3), (2, 1, 3, 1), (2, 1, 3, 2), (8, 2, 0, 3), (8, 2, 1, 3), (8, 2, 2, 3), (8, 2, 3, 3), (2, 2, 3, 1),
+    (2, 2, 3, 2), (9, 0, 0, 1), (5, 0, 0, 1), (9, 1, 0, 1), (5, 1, 0, 1), (9, 2, 0, 1), (5, 2, 0, 1), (9, 0, 1, 1),
+    (9, 1, 1, 1), (9, 2, 1, 1), (9, 0, 2, 1), (5, 0, 2, 1), (9, 1, 2, 1), (5, 1, 2, 1), (9, 2, 2, 1), (5, 2, 2, 1),
+    (9, 0, 3, 1), (9, 1, 3, 1), (9, 2, 3, 1), (9, 0, 0, 2), (9, 1, 0, 2), (9, 2, 0, 2), (9, 0, 1, 2), (5, 0, 1, 2),
+    (9, 1, 1, 2), (5, 1, 1, 2), (9, 2, 1, 2), (5, 2, 1, 2), (9, 0, 2, 2), (9, 1, 2, 2), (9, 2, 2, 2), (9, 0, 3, 2),
+    (5, 0, 3, 2), (9, 1, 3, 2), (5, 1, 3, 2), (9, 2, 3, 2), (5, 2, 3, 2), (10,), (9, 0, 0, 3), (9, 0, 1, 3),
+    (9, 0, 2, 3), (9, 2, 0, 3), (9, 2, 1, 3), (9, 2, 2, 3), (9, 2, 3, 3), (9, 0, 3, 3), (9, 1, 0, 3), (9, 1, 1, 3),
+    (9, 1, 2, 3), (9, 1, 3, 3),
 )
 STEPS = (0, -1, 1, 2)
 NT = (((1,), (1,)), ((), ()))
@@ -102,8 +102,8 @@
 
 
 def block_kernel(
-    frames, up, down, ffn_gain, final_gain, ctc_hbm, emis,
-    w, mine, ctc, x_in, normed_in, total,
+    frames, up, down, ffn_gain_hbm, final_gain_hbm, ctc_hbm, emis,
+    w, mine, ctc, ffn_gain, final_gain, x_in, normed_in, total,
     local_sem, fr_send, fr_recv, s1, r1, s2, r2, s3, r3, sc, rc,
 ):
     me = position()
@@ -113,7 +113,7 @@
 
     barrier = pltpu.get_barrier_semaphore()
     for axis in range(3):
-        for by in (1, -1):
+        for by in (1, -1, 2):
             pl.semaphore_signal(barrier, inc=1, device_id=device(*moved(me, axis, by)), device_id_type=MESH)
     pl.semaphore_signal(barrier, inc=1, device_id=sibling, device_id_type=MESH)
     for d in range(1, 8):
@@ -124,12 +124,14 @@
         pltpu.make_async_copy(down, here.at[pl.ds(80, 80)], local_sem.at[1]),
         pltpu.make_async_copy(frames.at[:, pl.ds(pl.multiple_of(chan * 256, 256), 256)], mine.at[chan], local_sem.at[2]),
         pltpu.make_async_copy(ctc_hbm, ctc, local_sem.at[3]),
+        pltpu.make_async_copy(ffn_gain_hbm, ffn_gain, local_sem.at[4]),
+        pltpu.make_async_copy(final_gain_hbm, final_gain, local_sem.at[5]),
     ]
     for copy in locals_:
         copy.start()
     locals_[0].wait()
     locals_[1].wait()
-    pl.semaphore_wait(barrier, 14)
+    pl.semaphore_wait(barrier, 17)
 
     pending = []
 
@@ -155,7 +157,7 @@
         return moved(pos, axis, STEPS[place])
 
     def send_to(ref, axis, q, send_sem, recv_sem):
-        send(ref, send_sem, recv_sem, device(*moved(me, axis, 1 if q == 1 else -1)))
+        send(ref, send_sem, recv_sem, device(*moved(me, axis, (1, -1, 2)[q - 1])))
 
     arrivals = {}
 
@@ -225,6 +227,7 @@
 
     def norm_frames():
         locals_[2].wait()
+        locals_[4].wait()
         for d in range(1, 8):
             arrived(mine.at[lax.rem(chan + 8 - d, 8)], fr_recv.at[d - 1])
         x_in[...] = jnp.transpose(mine[...].astype(jnp.float32).reshape(1280, 256))
@@ -267,6 +270,7 @@
     project(0, 4, 1 - x // 2)
 
     locals_[3].wait()
+    locals_[5].wait()
     residual = x_in[...] + 0.5 * total[...]
     normed = norm_rows(residual, gain_row(final_gain)).astype(jnp.bfloat16)
     logits = jnp.dot(normed, ctc[...], preferred_element_type=jnp.float32)
@@ -281,22 +285,24 @@
     return pl.pallas_call(
         block_kernel,
         out_shape=jax.ShapeDtypeStruct((256, 256), jnp.float32),
-        in_specs=[HBM, HBM, HBM, VM, VM, HBM],
+        in_specs=[HBM] * 6,
         out_specs=VM,
         scratch_shapes=[
             pltpu.VMEM((4, 2, 2, 4, 2, 160, 640), jnp.bfloat16),
             pltpu.VMEM((8, 160, 256), jnp.bfloat16),
             pltpu.VMEM((1280, 256), jnp.bfloat16),
+            pltpu.VMEM((10, 128), jnp.float32),
+            pltpu.VMEM((10, 128), jnp.float32),
             pltpu.VMEM((256, 1280), jnp.float32),
             pltpu.VMEM((256, 1280), jnp.bfloat16),
             pltpu.VMEM((256, 1280), jnp.float32),
-            dma((4,)), dma((7,)), dma((7,)),
+            dma((6,)), dma((7,)), dma((7,)),
             dma((3, 3)), dma((3, 4)),
             dma((3, 4, 3)), dma((3, 4, 4)),
             dma((3, 4, 3)), dma((3, 4, 4)),
             dma((3, 7)), dma((3, 7)),
         ],
-        compiler_params=pltpu.CompilerParams(collective_id=1, has_side_effects=True, vmem_limit_bytes=52 * MIB),
+        compiler_params=pltpu.CompilerParams(collective_id=1, has_side_effects=True, vmem_limit_bytes=62 * MIB),
         name="block",
     )(frames, up, down, ffn_gain, final_gain, ctc)
 

time: 116 us -> 112 us (0.966)
  local copies, waits for them, and re-layouts: 6.57 us -> 2.17 us
    unnamed x20 -> x10, local copies, waits for them, and re-layouts: 6.57 us -> 2.17 us
where the time goes in v4:
time: 112 us
  Pallas kernels  109 us (97%)
  local copies, waits for them, and re-layouts  2.17 us (2%)
    pallas_call x1, Pallas kernels, block_part(): pl.pallas_call(block_kernel, out_shape=jax.ShapeDtypeStruct((256, 256), j...  76.5 us
    pallas_call x1, Pallas kernels, path_part(): pl.pallas_call(path_kernel, out_shape=jax.ShapeDtypeStruct((1, 128), jnp....  32.7 us

profile of v4, /device:TPU:27, one launch (start us, length us, event | category | flops | bytes accessed | tf_op | source)
XLA Modules:
  0.0 112.0 jit_solution(9076079974895807614)
XLA Ops:
  0.6 0.0 copy-start.1
  0.6 0.0 copy-start.2
  0.7 0.0 copy-start.3
  0.7 76.5 %block.1.emissions = f32[256,256]{1,0:T(8,128)} custom-call(bf16[160,2048]{1,0:T(8,128)(2,1)} %bitcast.6, bf16[80,640]{1,0:T(8,128)(2,1)} %up.1, bf16[80,640]{1,0:T(8,128)(2,1)} %bitcast.7, f32[10,128]{1,0:T(8,128)} %bitcast.8, f32[10,128]{1,0:T(8,128)} %bitcast.9, bf16[1280,256]{1,0:T(8,128)(2,1)} %ctc_hbm.1), custom_call_target="tpu_custom_call" | custom-call | tf_op jit(solution)/shard_map/block/pallas_call | solution.py:285
  77.1 0.0 copy-done.1
  77.1 0.0 copy-done.2
  77.2 0.0 copy-done.3
  77.2 0.0 copy-start
  77.2 0.9 copy-done
  78.1 32.7 %path.1 = f32[1,128]{1,0:T(1,128)S(1)} custom-call(s32[128]{0:T(128)S(1)} %copy-done.2, s32[128]{0:T(128)S(1)} %copy-done.3, s32[64,128]{1,0:T(8,128)S(1)} %bitcast.5, f32[256,256]{1,0:T(8,128)S(1)} %copy-done), custom_call_target="tpu_custom_call" | custom-call | tf_op jit(solution)/shard_map/path/pallas_call | solution.py:495
  110.8 0.7 copy.13
  111.5 0.5 copy.14
Async XLA Ops:
  0.6 76.5 %copy-start.1 = (s32[8192]{0:T(1024)S(1)}, s32[8192]{0:T(1024)}, u32[]{:S(2)}) copy-start(s32[8192]{0:T(1024)} %param.15) | copy-start | bytes 98308
  0.6 76.5 %copy-start.2 = (s32[128]{0:T(128)S(1)}, s32[128]{0:T(128)}, u32[]{:S(2)}) copy-start(s32[128]{0:T(128)} %starts.1) | copy-start | bytes 1540
  0.7 76.5 %copy-start.3 = (s32[128]{0:T(128)S(1)}, s32[128]{0:T(128)}, u32[]{:S(2)}) copy-start(s32[128]{0:T(128)} %widths.1) | copy-start | bytes 1540
  77.2 1.0 copy-start

commit v5 on v4

--- a/solution.py
+++ b/solution.py
@@ -52,11 +52,11 @@
     (8, 2, 1, 2), (4, 2, 1, 2), (8, 2, 2, 2), (8, 2, 3, 2), (4, 2, 3, 2), (2, 2, 2, 1), (2, 2, 2, 2), (8, 0, 0, 3),
     (8, 0, 1, 3), (8, 0, 2, 3), (8, 0, 3, 3), (2, 0, 3, 1), (2, 0, 3, 2), (8, 1, 0, 3), (8, 1, 1, 3), (8, 1, 2, 3),
     (8, 1, 3, 3), (2, 1, 3, 1), (2, 1, 3, 2), (8, 2, 0, 3), (8, 2, 1, 3), (8, 2, 2, 3), (8, 2, 3, 3), (2, 2, 3, 1),
-    (2, 2, 3, 2), (9, 0, 0, 1), (5, 0, 0, 1), (9, 1, 0, 1), (5, 1, 0, 1), (9, 2, 0, 1), (5, 2, 0, 1), (9, 0, 1, 1),
-    (9, 1, 1, 1), (9, 2, 1, 1), (9, 0, 2, 1), (5, 0, 2, 1), (9, 1, 2, 1), (5, 1, 2, 1), (9, 2, 2, 1), (5, 2, 2, 1),
-    (9, 0, 3, 1), (9, 1, 3, 1), (9, 2, 3, 1), (9, 0, 0, 2), (9, 1, 0, 2), (9, 2, 0, 2), (9, 0, 1, 2), (5, 0, 1, 2),
-    (9, 1, 1, 2), (5, 1, 1, 2), (9, 2, 1, 2), (5, 2, 1, 2), (9, 0, 2, 2), (9, 1, 2, 2), (9, 2, 2, 2), (9, 0, 3, 2),
-    (5, 0, 3, 2), (9, 1, 3, 2), (5, 1, 3, 2), (9, 2, 3, 2), (5, 2, 3, 2), (10,), (9, 0, 0, 3), (9, 0, 1, 3),
+    (2, 2, 3, 2), (9, 0, 0, 1), (5, 0, 0, 1), (9, 0, 0, 2), (9, 1, 0, 1), (5, 1, 0, 1), (9, 1, 0, 2), (9, 2, 0, 1),
+    (5, 2, 0, 1), (9, 2, 0, 2), (9, 0, 1, 1), (9, 0, 1, 2), (5, 0, 1, 2), (9, 1, 1, 1), (9, 1, 1, 2), (5, 1, 1, 2),
+    (9, 2, 1, 1), (9, 2, 1, 2), (5, 2, 1, 2), (9, 0, 2, 1), (5, 0, 2, 1), (9, 0, 2, 2), (9, 1, 2, 1), (5, 1, 2, 1),
+    (9, 1, 2, 2), (9, 2, 2, 1), (5, 2, 2, 1), (9, 2, 2, 2), (9, 0, 3, 1), (9, 0, 3, 2), (5, 0, 3, 2), (9, 1, 3, 1),
+    (9, 1, 3, 2), (5, 1, 3, 2), (9, 2, 3, 1), (9, 2, 3, 2), (5, 2, 3, 2), (10,), (9, 0, 0, 3), (9, 0, 1, 3),
     (9, 0, 2, 3), (9, 2, 0, 3), (9, 2, 1, 3), (9, 2, 2, 3), (9, 2, 3, 3), (9, 0, 3, 3), (9, 1, 0, 3), (9, 1, 1, 3),
     (9, 1, 2, 3), (9, 1, 3, 3),
 )
@@ -383,16 +383,14 @@
 
     @pl.when(root)
     def _():
+        members = [lax.rem(chan + d, 8) for d in range(8)]
+
         def greet(g, carry):
-            for d in range(8):
-
-                @pl.when(jnp.logical_or(g != 0, d != 0))
-                def _():
-                    pl.semaphore_signal(barrier, inc=1, device_id=(g, lax.rem(chan + d, 8)), device_id_type=MESH)
-
+            for member in members:
+                pl.semaphore_signal(barrier, inc=1, device_id=(g, member), device_id_type=MESH)
             return carry
 
-        lax.fori_loop(0, 16, greet, 0)
+        lax.fori_loop(1, 16, greet, 0)
 
     @pl.when(jnp.logical_not(root))
     def _():
@@ -408,7 +406,7 @@
 
     @pl.when(root)
     def _():
-        pl.semaphore_wait(barrier, 7 + 7 + 15)
+        pl.semaphore_wait(barrier, 7 + 15)
 
     @pl.when(jnp.logical_not(root))
     def _():
@@ -417,18 +415,23 @@
     copies = []
     for d in range(1, 8):
         copy = pltpu.make_async_remote_copy(
-            src_ref=transfer, dst_ref=group.at[chan], send_sem=ts.at[d - 1], recv_sem=tr.at[d - 1],
+            src_ref=transfer, dst_ref=group.at[chan], send_sem=ts.at[d - 1], recv_sem=tr.at[chan],
             device_id=(tm, lax.rem(chan + d, 8)), device_id_type=MESH,
         )
         copy.start()
         copies.append(copy)
     group[chan] = transfer[...]
-    for copy in copies:
-        copy.wait_recv()
-
+
+    def await_member(m):
+        @pl.when(m != chan)
+        def _():
+            pltpu.make_async_copy(group.at[m], group.at[m], tr.at[m]).wait()
+
+    await_member(0)
     span = group[0, pl.ds(pl.multiple_of(chan * 16, 16), 16), :]
 
     def grow(m, span):
+        await_member(m)
         best = span[:, 0:1] + group[m, 0:1, :]
         for i in range(1, 128):
             best = jnp.maximum(best, span[:, i : i + 1] + group[m, i : i + 1, :])
@@ -505,7 +508,7 @@
             pltpu.VMEM((2048, 128), jnp.float32),
             pltpu.VMEM((8, 128), jnp.float32),
             pltpu.VMEM((16, 8, 128), jnp.float32),
-            dma((7,)), dma((7,)), dma((8,)), dma, dma((16,)), dma,
+            dma((7,)), dma((8,)), dma((8,)), dma, dma((16,)), dma,
         ],
         compiler_params=pltpu.CompilerParams(collective_id=2, has_side_effects=True, vmem_limit_bytes=24 * MIB),
         name="path",

time: 112 us -> 112 us (level)
  no operation moved by 1% of the time
where the time goes in v5:
time: 112 us
  Pallas kernels  109 us (97%)
  local copies, waits for them, and re-layouts  2.17 us (2%)
    pallas_call x1, Pallas kernels, block_part(): pl.pallas_call(block_kernel, out_shape=jax.ShapeDtypeStruct((256, 256), j...  76 us
    pallas_call x1, Pallas kernels, path_part(): pl.pallas_call(path_kernel, out_shape=jax.ShapeDtypeStruct((1, 128), jnp....  32.6 us

profile of v5, /device:TPU:27, one launch (start us, length us, event | category | flops | bytes accessed | tf_op | source)
XLA Modules:
  0.0 111.5 jit_solution(15293812166598132020)
XLA Ops:
  0.6 0.0 copy-start.1
  0.6 0.0 copy-start.2
  0.7 0.0 copy-start.3
  0.7 76.0 %block.1.emissions = f32[256,256]{1,0:T(8,128)} custom-call(bf16[160,2048]{1,0:T(8,128)(2,1)} %bitcast.6, bf16[80,640]{1,0:T(8,128)(2,1)} %up.1, bf16[80,640]{1,0:T(8,128)(2,1)} %bitcast.7, f32[10,128]{1,0:T(8,128)} %bitcast.8, f32[10,128]{1,0:T(8,128)} %bitcast.9, bf16[1280,256]{1,0:T(8,128)(2,1)} %ctc_hbm.1), custom_call_target="tpu_custom_call" | custom-call | tf_op jit(solution)/shard_map/block/pallas_call | solution.py:285
  76.7 0.0 copy-done.1
  76.7 0.0 copy-done.2
  76.7 0.0 copy-done.3
  76.7 0.0 copy-start
  76.8 0.9 copy-done
  77.7 32.6 %path.1 = f32[1,128]{1,0:T(1,128)S(1)} custom-call(s32[128]{0:T(128)S(1)} %copy-done.2, s32[128]{0:T(128)S(1)} %copy-done.3, s32[64,128]{1,0:T(8,128)S(1)} %bitcast.5, f32[256,256]{1,0:T(8,128)S(1)} %copy-done), custom_call_target="tpu_custom_call" | custom-call | tf_op jit(solution)/shard_map/path/pallas_call | solution.py:498
  110.3 0.7 copy.13
  111.0 0.5 copy.14
Async XLA Ops:
  0.6 76.1 %copy-start.1 = (s32[8192]{0:T(1024)S(1)}, s32[8192]{0:T(1024)}, u32[]{:S(2)}) copy-start(s32[8192]{0:T(1024)} %param.15) | copy-start | bytes 98308
  0.6 76.1 %copy-start.2 = (s32[128]{0:T(128)S(1)}, s32[128]{0:T(128)}, u32[]{:S(2)}) copy-start(s32[128]{0:T(128)} %starts.1) | copy-start | bytes 1540
  0.7 76.1 %copy-start.3 = (s32[128]{0:T(128)S(1)}, s32[128]{0:T(128)}, u32[]{:S(2)}) copy-start(s32[128]{0:T(128)} %widths.1) | copy-start | bytes 1540
  76.7 1.0 copy-start

commit v6 on v5

--- a/solution.py
+++ b/solution.py
@@ -38,7 +38,7 @@
 )
 ALL = (0, 1, 2)
 ORDER = (
-    (0, 0, 1), (0, 0, 2), (0, 0, 3), (0, 1, 1), (0, 1, 2), (0, 1, 3), (0, 2, 1), (0, 2, 2), (0, 2, 3), (1, 0, 0, 1),
+    (0, 0, 3), (0, 1, 3), (0, 2, 3), (0, 0, 1), (0, 0, 2), (0, 1, 1), (0, 1, 2), (0, 2, 1), (0, 2, 2), (1, 0, 0, 1),
     (1, 0, 0, 2), (1, 1, 0, 1), (1, 1, 0, 2), (1, 2, 0, 1), (1, 2, 0, 2), (7, 0, 1), (1, 0, 1, 1), (1, 0, 1, 2),
     (7, 1, 1), (1, 1, 1, 1), (1, 1, 1, 2), (7, 2, 1), (1, 2, 1, 1), (1, 2, 1, 2), (7, 0, 2), (1, 0, 2, 1),
     (1, 0, 2, 2), (7, 1, 2), (1, 1, 2, 1), (1, 1, 2, 2), (7, 2, 2), (1, 2, 2, 1), (1, 2, 2, 2), (7, 0, 3),

time: 112 us -> 112 us (level)
  no operation moved by 1% of the time
where the time goes in v6:
time: 112 us
  Pallas kernels  109 us (97%)
  local copies, waits for them, and re-layouts  2.17 us (2%)
    pallas_call x1, Pallas kernels, block_part(): pl.pallas_call(block_kernel, out_shape=jax.ShapeDtypeStruct((256, 256), j...  76 us
    pallas_call x1, Pallas kernels, path_part(): pl.pallas_call(path_kernel, out_shape=jax.ShapeDtypeStruct((1, 128), jnp....  33.3 us

profile of v6, /device:TPU:27, one launch (start us, length us, event | category | flops | bytes accessed | tf_op | source)
XLA Modules:
  0.0 112.3 jit_solution(15429584315127296645)
XLA Ops:
  0.6 0.0 copy-start.1
  0.6 0.0 copy-start.2
  0.7 0.0 copy-start.3
  0.7 76.0 %block.1.emissions = f32[256,256]{1,0:T(8,128)} custom-call(bf16[160,2048]{1,0:T(8,128)(2,1)} %bitcast.6, bf16[80,640]{1,0:T(8,128)(2,1)} %up.1, bf16[80,640]{1,0:T(8,128)(2,1)} %bitcast.7, f32[10,128]{1,0:T(8,128)} %bitcast.8, f32[10,128]{1,0:T(8,128)} %bitcast.9, bf16[1280,256]{1,0:T(8,128)(2,1)} %ctc_hbm.1), custom_call_target="tpu_custom_call" | custom-call | tf_op jit(solution)/shard_map/block/pallas_call | solution.py:285
  76.7 0.0 copy-done.1
  76.7 0.0 copy-done.2
  76.7 0.0 copy-done.3
  76.7 0.0 copy-start
  76.8 0.9 copy-done
  77.7 33.3 %path.1 = f32[1,128]{1,0:T(1,128)S(1)} custom-call(s32[128]{0:T(128)S(1)} %copy-done.2, s32[128]{0:T(128)S(1)} %copy-done.3, s32[64,128]{1,0:T(8,128)S(1)} %bitcast.5, f32[256,256]{1,0:T(8,128)S(1)} %copy-done), custom_call_target="tpu_custom_call" | custom-call | tf_op jit(solution)/shard_map/path/pallas_call | solution.py:498
  111.0 0.7 copy.13
  111.7 0.5 copy.14
Async XLA Ops:
  0.6 76.1 %copy-start.1 = (s32[8192]{0:T(1024)S(1)}, s32[8192]{0:T(1024)}, u32[]{:S(2)}) copy-start(s32[8192]{0:T(1024)} %param.15) | copy-start | bytes 98308
  0.6 76.1 %copy-start.2 = (s32[128]{0:T(128)S(1)}, s32[128]{0:T(128)}, u32[]{:S(2)}) copy-start(s32[128]{0:T(128)} %starts.1) | copy-start | bytes 1540
  0.7 76.1 %copy-start.3 = (s32[128]{0:T(128)S(1)}, s32[128]{0:T(128)}, u32[]{:S(2)}) copy-start(s32[128]{0:T(128)} %widths.1) | copy-start | bytes 1540
  76.7 1.0 copy-start
